TPU v7x, 32 devices: a whole 2x2x4 slice. The times are simulated.
32 devices in a mesh: dp: 4 (over x, core), feat: 8 (over z, y).
Axes of the slice: x: 2, y: 2, z: 4, core: 2. Of those that a mesh axis runs over, the one named last changes fastest.
Arguments:
- tokens: bfloat16 [512, 16384], P('dp', 'feat'), may hold values from -6 to 6
- cotangent: bfloat16 [512, 16384], P('dp', 'feat'), may hold values from -6 to 6
- factor_in: bfloat16 [7, 128, 2, 128, 128], P(None, 'feat', None, 'dp'), may hold values from -0.375 to 0.375
- factor_out: bfloat16 [7, 128, 2, 128, 128], P(None, 'feat', None, 'dp'), may hold values from -0.375 to 0.375
Outputs:
- outputs: bfloat16 [512, 16384], P('dp', 'feat')
- token_grad: bfloat16 [512, 16384], P('dp', 'feat')
- factor_in_grad: float32 [7, 128, 2, 128, 128], P(None, 'feat', None, 'dp')
- factor_out_grad: float32 [7, 128, 2, 128, 128], P(None, 'feat', None, 'dp')
All inputs are finite; a program needn't handle non-finite values.
Results may differ from a plain program's by a relative error of at most 0.035.
Values may be sent and summed in bfloat16 or wider, within the bound.
A program may use at most 128 MiB of HBM per device.

v0:
```python
import math

import jax
import jax.numpy as jnp
from jax import lax
from jax.sharding import PartitionSpec as P


def partner_2(value, axis, stride):
    mask = 2**stride
    pairs = [(source, source ^ mask) for source in range(lax.axis_size(axis))]
    return lax.ppermute(value, axis, pairs)


def flip_blocks(values, bit_no):
    row_count, block_count, block_cols = values.shape
    span = 2**bit_no
    grouped = values.reshape(row_count, block_count // (2 * span), 2, span, block_cols)
    return jnp.flip(grouped, 2).reshape(row_count, block_count, block_cols)


def act_partner(values, bit_no, local_bits):
    if bit_no < local_bits:
        return flip_blocks(values, bit_no)
    return partner_2(values, "feat", bit_no - local_bits)


def grad_partner(values, bit_no, local_bits):
    if bit_no < local_bits:
        return flip_blocks(values, bit_no)
    return partner_2(values, "feat", bit_no - local_bits)


def gelu_exact(pre_act):
    return 0.5 * pre_act * (1.0 + lax.erf(pre_act * 0.7071067811865476))


def gelu_slope(pre_act):
    return (
        0.5 * (1.0 + lax.erf(pre_act * 0.7071067811865476))
        + pre_act * jnp.exp(-0.5 * pre_act * pre_act) * 0.3989422804014327
    )


def apply_level(values, partner, factor):
    own_term = jnp.einsum("tjr,jrc->tjc", values, factor[:, 0], preferred_element_type=jnp.float32)
    other_term = jnp.einsum(
        "tjr,jrc->tjc", partner, factor[:, 1], preferred_element_type=jnp.float32
    )
    return own_term + other_term


def gather_level(factor_shard):
    return lax.all_gather(factor_shard, "dp", axis=2, tiled=True)


def sum_level(level_grad):
    return lax.psum_scatter(
        level_grad.astype(jnp.bfloat16), "dp", scatter_dimension=2, tiled=True
    ).astype(jnp.float32)


def forward_map(current, factors, local_bits, last_plain):
    stored = []
    for layer_no in range(len(factors)):
        partner = act_partner(current, layer_no, local_bits)
        stored.append((current, partner))
        summed = apply_level(current, partner, factors[layer_no])
        if layer_no < len(factors) - 1 or not last_plain:
            current = summed.astype(jnp.bfloat16)
    return (summed, current, stored)


def backward_map(grad_in, stored, factors, local_bits, grad_scale):
    level_grads = [None] * len(factors)
    current = grad_in
    for layer_no in reversed(range(len(factors))):
        values, partner = stored[layer_no]
        factor = factors[layer_no]
        d_self = jnp.einsum("tjr,tjc->jrc", values, current, preferred_element_type=jnp.float32)
        d_part = jnp.einsum("tjr,tjc->jrc", partner, current, preferred_element_type=jnp.float32)
        level_grad = jnp.stack([d_self, d_part], 1) * grad_scale
        level_grads[layer_no] = sum_level(level_grad)
        outgoing = jnp.einsum(
            "tjc,jrc->tjr", current, factor[:, 1], preferred_element_type=jnp.float32
        ).astype(jnp.bfloat16)
        incoming = grad_partner(outgoing, layer_no, local_bits)
        own_term = jnp.einsum(
            "tjc,jrc->tjr", current, factor[:, 0], preferred_element_type=jnp.float32
        )
        current = (own_term + incoming.astype(jnp.float32)).astype(jnp.bfloat16)
    stacked = jnp.stack(level_grads, 0)
    return (current, stacked)


def on_device(tokens, cotangent, factor_in, factor_out):
    level_count = factor_in.shape[0]
    block_cols = factor_in.shape[4]
    local_blocks = factor_in.shape[1]
    local_bits = local_blocks.bit_length() - 1
    tok_rows = tokens.shape[0]
    grad_scale = 1.0 / math.sqrt(tok_rows * lax.axis_size("dp"))
    factors_first = [gather_level(factor_in[layer_no]) for layer_no in range(level_count)]
    factors_second = [gather_level(factor_out[layer_no]) for layer_no in range(level_count)]
    current = tokens.reshape(tok_rows, local_blocks, block_cols)
    pre_gelu, unused_last, stored_in = forward_map(current, factors_first, local_bits, True)
    hidden = gelu_exact(pre_gelu).astype(jnp.bfloat16)
    unused_sum, mapped, stored_out = forward_map(hidden, factors_second, local_bits, False)
    outputs = mapped.reshape(tok_rows, local_blocks * block_cols)
    grad_mid, factor_out_grad = backward_map(
        cotangent.reshape(tok_rows, local_blocks, block_cols),
        stored_out,
        factors_second,
        local_bits,
        grad_scale,
    )
    grad_pre = (grad_mid.astype(jnp.float32) * gelu_slope(pre_gelu)).astype(jnp.bfloat16)
    token_grad, factor_in_grad = backward_map(
        grad_pre, stored_in, factors_first, local_bits, grad_scale
    )
    return (
        outputs,
        token_grad.reshape(tok_rows, local_blocks * block_cols),
        factor_in_grad,
        factor_out_grad,
    )


def solution(mesh):
    placed = (
        P("dp", "feat"),
        P("dp", "feat"),
        P(None, "feat", None, "dp", None),
        P(None, "feat", None, "dp", None),
    )
    return jax.shard_map(
        on_device,
        mesh=mesh,
        in_specs=placed,
        out_specs=(
            P("dp", "feat"),
            P("dp", "feat"),
            P(None, "feat", None, "dp", None),
            P(None, "feat", None, "dp", None),
        ),
        check_vma=False,
    )
```

profile of v0, /device:TPU:0, one launch (start us, length us, event | category | flops | bytes accessed | tf_op | source)
XLA Modules:
  0.0 664.3 jit_solution(280134519645268801)
XLA Ops:
  7.2 2.7 fusion.112
  26.0 2.9 rev.52
  33.4 15.9 %all-gather.31.cloned.1.call-done = bf16[1,16,2,128,128]{4,3,1,2,0:T(8,128)(2,1)} async-done(((bf16[1,16,2,32,128]{4,3,1,2,0:T(8,128)(2,1)}), bf16[1,16,2,128,128]{4,3,1,2,0:T(8,128)(2,1)}) %all-gather.31.cloned.1.call-update) | async-done | bytes 1048592 | tf_op jit(solution)/shard_map/all_gather | solution.py:54
  51.2 17.0 %all-gather.33.cloned.1.call-done = bf16[1,16,2,128,128]{4,3,1,2,0:T(8,128)(2,1)} async-done(((bf16[1,16,2,32,128]{4,3,1,2,0:T(8,128)(2,1)}), bf16[1,16,2,128,128]{4,3,1,2,0:T(8,128)(2,1)}) %all-gather.33.cloned.1.call-update) | async-done | bytes 1048592 | tf_op jit(solution)/shard_map/all_gather | solution.py:54
  70.0 16.3 %all-gather.35.cloned.1.call-done = bf16[1,16,2,128,128]{4,3,1,2,0:T(8,128)(2,1)} async-done(((bf16[1,16,2,32,128]{4,3,1,2,0:T(8,128)(2,1)}), bf16[1,16,2,128,128]{4,3,1,2,0:T(8,128)(2,1)}) %all-gather.35.cloned.1.call-update) | async-done | bytes 1048592 | tf_op jit(solution)/shard_map/all_gather | solution.py:54
  88.7 15.9 %all-gather.55.cloned.1.call-done = bf16[1,16,2,128,128]{4,1,2,0,3:T(8,128)(2,1)} async-done(((bf16[1,16,2,32,128]{4,1,2,0,3:T(8,128)(2,1)}), bf16[1,16,2,128,128]{4,1,2,0,3:T(8,128)(2,1)}) %all-gather.55.cloned.1.call-update) | async-done | bytes 1048592 | tf_op jit(solution)/shard_map/all_gather | solution.py:54
  107.1 2.5 collective-permute-start.6
  112.4 10.3 %all-gather.37.cloned.1.call-done = bf16[1,16,2,128,128]{4,3,1,2,0:T(8,128)(2,1)} async-done(((bf16[1,16,2,32,128]{4,3,1,2,0:T(8,128)(2,1)}), bf16[1,16,2,128,128]{4,3,1,2,0:T(8,128)(2,1)}) %all-gather.37.cloned.1.call-update) | async-done | bytes 1048592 | tf_op jit(solution)/shard_map/all_gather | solution.py:54
  125.0 8.4 %collective-permute-done.6 = bf16[128,16,128]{0,2,1:T(8,128)(2,1)} collective-permute-done((bf16[128,16,128]{0,2,1:T(8,128)(2,1)S(1)}, bf16[128,16,128]{0,2,1:T(8,128)(2,1)}, u32[]{:S(2)}, u32[]{:S(2)}) %collective-permute-start.6) | collective-permute-done | bytes 524320 | tf_op jit(solution)/shard_map/ppermute | solution.py:12
  135.0 6.1 all-gather.53.cloned.1.call-done
  146.4 13.6 %all-gather.39.cloned.1.call-done = bf16[1,16,2,128,128]{4,3,1,2,0:T(8,128)(2,1)} async-done(((bf16[1,16,2,32,128]{4,3,1,2,0:T(8,128)(2,1)}), bf16[1,16,2,128,128]{4,3,1,2,0:T(8,128)(2,1)}) %all-gather.39.cloned.1.call-update) | async-done | bytes 1048592 | tf_op jit(solution)/shard_map/all_gather | solution.py:54
  164.0 14.3 %all-gather.51.cloned.1.call-done = bf16[1,16,2,128,128]{4,3,1,2,0:T(8,128)(2,1)} async-done(((bf16[1,16,2,32,128]{4,3,1,2,0:T(8,128)(2,1)}), bf16[1,16,2,128,128]{4,3,1,2,0:T(8,128)(2,1)}) %all-gather.51.cloned.1.call-update) | async-done | bytes 1048592 | tf_op jit(solution)/shard_map/all_gather | solution.py:54
  178.3 2.4 fusion.61
  183.7 2.5 collective-permute-start.2
  186.2 10.3 %all-gather.41.cloned.1.call-done = bf16[1,16,2,128,128]{4,3,1,2,0:T(8,128)(2,1)} async-done(((bf16[1,16,2,32,128]{4,3,1,2,0:T(8,128)(2,1)}), bf16[1,16,2,128,128]{4,3,1,2,0:T(8,128)(2,1)}) %all-gather.41.cloned.1.call-update) | async-done | bytes 1048592 | tf_op jit(solution)/shard_map/all_gather | solution.py:54
  200.4 14.3 %all-gather.49.cloned.1.call-done = bf16[1,16,2,128,128]{4,3,1,2,0:T(8,128)(2,1)} async-done(((bf16[1,16,2,32,128]{4,3,1,2,0:T(8,128)(2,1)}), bf16[1,16,2,128,128]{4,3,1,2,0:T(8,128)(2,1)}) %all-gather.49.cloned.1.call-update) | async-done | bytes 1048592 | tf_op jit(solution)/shard_map/all_gather | solution.py:54
  217.1 3.0 multiply_convert_fusion
  221.5 11.5 %all-gather.47.cloned.1.call-done = bf16[1,16,2,128,128]{4,3,1,2,0:T(8,128)(2,1)} async-done(((bf16[1,16,2,32,128]{4,3,1,2,0:T(8,128)(2,1)}), bf16[1,16,2,128,128]{4,3,1,2,0:T(8,128)(2,1)}) %all-gather.47.cloned.1.call-update) | async-done | bytes 1048592 | tf_op jit(solution)/shard_map/all_gather | solution.py:54
  238.8 12.4 %all-gather.45.cloned.1.call-done = bf16[1,16,2,128,128]{4,3,1,2,0:T(8,128)(2,1)} async-done(((bf16[1,16,2,32,128]{4,3,1,2,0:T(8,128)(2,1)}), bf16[1,16,2,128,128]{4,3,1,2,0:T(8,128)(2,1)}) %all-gather.45.cloned.1.call-update) | async-done | bytes 1048592 | tf_op jit(solution)/shard_map/all_gather | solution.py:54
  259.8 2.7 copy.183
  262.8 6.7 %all-gather.43.cloned.1.call-done = bf16[1,16,2,128,128]{4,3,1,2,0:T(8,128)(2,1)} async-done(((bf16[1,16,2,32,128]{4,3,1,2,0:T(8,128)(2,1)}), bf16[1,16,2,128,128]{4,3,1,2,0:T(8,128)(2,1)}) %all-gather.43.cloned.1.call-update) | async-done | bytes 1048592 | tf_op jit(solution)/shard_map/all_gather | solution.py:54
  277.3 2.8 copy.187
  285.6 2.7 copy.191
  293.3 2.8 copy.195
  308.4 8.0 %collective-permute-done.3 = bf16[128,16,128]{2,0,1:T(8,128)(2,1)S(1)} collective-permute-done((bf16[128,16,128]{2,0,1:T(8,128)(2,1)S(1)}, bf16[128,16,128]{2,0,1:T(8,128)(2,1)S(1)}, u32[]{:S(2)}, u32[]{:S(2)}) %collective-permute-start.3) | collective-permute-done | bytes 524320 | tf_op jit(solution)/shard_map/ppermute | solution.py:12
  318.8 2.7 copy.200
  321.9 9.7 %collective-permute-done.9 = bf16[128,16,128]{2,0,1:T(8,128)(2,1)} collective-permute-done((bf16[128,16,128]{2,0,1:T(8,128)(2,1)S(1)}, bf16[128,16,128]{2,0,1:T(8,128)(2,1)}, u32[]{:S(2)}, u32[]{:S(2)}) %collective-permute-start.9) | collective-permute-done | bytes 524320 | tf_op jit(solution)/shard_map/ppermute | solution.py:12
  337.7 12.1 %collective-permute-done.10 = bf16[128,16,128]{2,0,1:T(8,128)(2,1)S(1)} collective-permute-done((bf16[128,16,128]{2,0,1:T(8,128)(2,1)S(1)}, bf16[128,16,128]{2,0,1:T(8,128)(2,1)S(1)}, u32[]{:S(2)}, u32[]{:S(2)}) %collective-permute-start.10) | collective-permute-done | bytes 524320 | tf_op jit(solution)/shard_map/ppermute | solution.py:12
  352.4 6.7 %collective-permute-done.4 = bf16[128,16,128]{2,0,1:T(8,128)(2,1)S(1)} collective-permute-done((bf16[128,16,128]{2,0,1:T(8,128)(2,1)S(1)}, bf16[128,16,128]{2,0,1:T(8,128)(2,1)S(1)}, u32[]{:S(2)}, u32[]{:S(2)}) %collective-permute-start.4) | collective-permute-done | bytes 524320 | tf_op jit(solution)/shard_map/ppermute | solution.py:12
  378.4 2.7 copy.146
  384.8 2.7 copy.149
  390.7 2.6 copy.153
  396.5 2.8 copy.157
  413.7 4.2 collective-permute-start.5
  417.9 2.4 convolution_bitcast_fusion.3
  420.3 2.5 fusion.104
  432.3 7.9 %collective-permute-done.5 = bf16[128,16,128]{2,0,1:T(8,128)(2,1)} collective-permute-done((bf16[128,16,128]{2,0,1:T(8,128)(2,1)}, bf16[128,16,128]{2,0,1:T(8,128)(2,1)}, u32[]{:S(2)}, u32[]{:S(2)}) %collective-permute-start.5) | collective-permute-done | bytes 524320 | tf_op jit(solution)/shard_map/ppermute | solution.py:12
  442.9 2.8 copy.214
  454.9 6.6 reduce-scatter.15.cloned.1.call-done
  463.2 25.9 %reduce-scatter.17.cloned.1.call-done = bf16[16,2,32,128]{3,0,1,2:T(8,128)(2,1)} async-done(((bf16[16,2,128,128]{3,0,1,2:T(8,128)(2,1)}), bf16[16,2,32,128]{3,0,1,2:T(8,128)(2,1)}) %reduce-scatter.17.cloned.1.call-update) | async-done | bytes 262160 | tf_op jit(solution)/shard_map/reduce_scatter | solution.py:58
  490.8 25.7 %reduce-scatter.19.cloned.1.call-done = bf16[16,2,32,128]{3,0,1,2:T(8,128)(2,1)} async-done(((bf16[16,2,128,128]{3,0,1,2:T(8,128)(2,1)}), bf16[16,2,32,128]{3,0,1,2:T(8,128)(2,1)}) %reduce-scatter.19.cloned.1.call-update) | async-done | bytes 262160 | tf_op jit(solution)/shard_map/reduce_scatter | solution.py:58
  518.2 25.8 %reduce-scatter.21.cloned.1.call-done = bf16[16,2,32,128]{3,0,1,2:T(8,128)(2,1)} async-done(((bf16[16,2,128,128]{3,0,1,2:T(8,128)(2,1)}), bf16[16,2,32,128]{3,0,1,2:T(8,128)(2,1)}) %reduce-scatter.21.cloned.1.call-update) | async-done | bytes 262160 | tf_op jit(solution)/shard_map/reduce_scatter | solution.py:58
  545.7 25.7 %reduce-scatter.23.cloned.1.call-done = bf16[16,2,32,128]{3,0,1,2:T(8,128)(2,1)} async-done(((bf16[16,2,128,128]{3,0,1,2:T(8,128)(2,1)}), bf16[16,2,32,128]{3,0,1,2:T(8,128)(2,1)}) %reduce-scatter.23.cloned.1.call-update) | async-done | bytes 262160 | tf_op jit(solution)/shard_map/reduce_scatter | solution.py:58
  573.2 25.8 %reduce-scatter.25.cloned.1.call-done = bf16[16,2,32,128]{3,0,1,2:T(8,128)(2,1)} async-done(((bf16[16,2,128,128]{3,0,1,2:T(8,128)(2,1)}), bf16[16,2,32,128]{3,0,1,2:T(8,128)(2,1)}) %reduce-scatter.25.cloned.1.call-update) | async-done | bytes 262160 | tf_op jit(solution)/shard_map/reduce_scatter | solution.py:58
  600.7 25.5 %reduce-scatter.27.cloned.1.call-done = bf16[16,2,32,128]{3,0,1,2:T(8,128)(2,1)} async-done(((bf16[16,2,128,128]{3,0,1,2:T(8,128)(2,1)}), bf16[16,2,32,128]{3,0,1,2:T(8,128)(2,1)}) %reduce-scatter.27.cloned.1.call-update) | async-done | bytes 262160 | tf_op jit(solution)/shard_map/reduce_scatter | solution.py:58
  628.0 3.9 stack.223
  631.8 22.0 %reduce-scatter.41.cloned.1.call-done = bf16[16,2,32,128]{3,0,1,2:T(8,128)(2,1)} async-done(((bf16[16,2,128,128]{3,0,1,2:T(8,128)(2,1)}), bf16[16,2,32,128]{3,0,1,2:T(8,128)(2,1)}) %reduce-scatter.41.cloned.1.call-update) | async-done | bytes 262160 | tf_op jit(solution)/shard_map/reduce_scatter | solution.py:58
  654.9 2.4 stack.253
  (377 shorter events, 189.9 us)
Async XLA Ops:
  7.2 99.4 %copy-start = (bf16[128,2048]{1,0:T(8,128)(2,1)S(1)}, bf16[128,2048]{1,0:T(8,128)(2,1)}, u32[]{:S(2)}) copy-start(bf16[128,2048]{1,0:T(8,128)(2,1)} %param.5) | copy-start | bytes 1572868
  7.2 23.2 %all-gather.29.cloned.1.call-start = ((), (), s32[]{:S(2)}) async-start(), calls=%async_computation.28 | async-start | bytes 1310720 | tf_op jit(solution)/shard_map/all_gather | solution.py:54
  10.8 38.5 %all-gather.31.cloned.1.call-start = ((), (), s32[]{:S(2)}) async-start(), calls=%async_computation.29 | async-start | bytes 1310720 | tf_op jit(solution)/shard_map/all_gather | solution.py:54
  12.6 55.6 %all-gather.33.cloned.1.call-start = ((), (), s32[]{:S(2)}) async-start(), calls=%async_computation.30 | async-start | bytes 1310720 | tf_op jit(solution)/shard_map/all_gather | solution.py:54
  13.4 73.0 %all-gather.35.cloned.1.call-start = ((), (), s32[]{:S(2)}) async-start(), calls=%async_computation.31 | async-start | bytes 1310720 | tf_op jit(solution)/shard_map/all_gather | solution.py:54
  14.2 90.4 %all-gather.55.cloned.1.call-start = ((), (), s32[]{:S(2)}) async-start(), calls=%async_computation.41 | async-start | bytes 1310720 | tf_op jit(solution)/shard_map/all_gather | solution.py:54
  16.4 106.3 %all-gather.37.cloned.1.call-start = ((), (), s32[]{:S(2)}) async-start(), calls=%async_computation.32 | async-start | bytes 1310720 | tf_op jit(solution)/shard_map/all_gather | solution.py:54
  18.2 122.9 %all-gather.53.cloned.1.call-start = ((), (), s32[]{:S(2)}) async-start(), calls=%async_computation.40 | async-start | bytes 1310720 | tf_op jit(solution)/shard_map/all_gather | solution.py:54
  19.9 140.0 %all-gather.39.cloned.1.call-start = ((), (), s32[]{:S(2)}) async-start(), calls=%async_computation.33 | async-start | bytes 1310720 | tf_op jit(solution)/shard_map/all_gather | solution.py:54
  20.7 157.5 %all-gather.51.cloned.1.call-start = ((), (), s32[]{:S(2)}) async-start(), calls=%async_computation.39 | async-start | bytes 1310720 | tf_op jit(solution)/shard_map/all_gather | solution.py:54
  21.5 174.9 %all-gather.41.cloned.1.call-start = ((), (), s32[]{:S(2)}) async-start(), calls=%async_computation.34 | async-start | bytes 1310720 | tf_op jit(solution)/shard_map/all_gather | solution.py:54
  22.3 192.5 %all-gather.49.cloned.1.call-start = ((), (), s32[]{:S(2)}) async-start(), calls=%async_computation.38 | async-start | bytes 1310720 | tf_op jit(solution)/shard_map/all_gather | solution.py:54
  23.1 209.8 %all-gather.47.cloned.1.call-start = ((), (), s32[]{:S(2)}) async-start(), calls=%async_computation.37 | async-start | bytes 1310720 | tf_op jit(solution)/shard_map/all_gather | solution.py:54
  23.9 227.3 %all-gather.45.cloned.1.call-start = ((), (), s32[]{:S(2)}) async-start(), calls=%async_computation.36 | async-start | bytes 1310720 | tf_op jit(solution)/shard_map/all_gather | solution.py:54
  24.7 244.7 %all-gather.43.cloned.1.call-start = ((), (), s32[]{:S(2)}) async-start(), calls=%async_computation.35 | async-start | bytes 1310720 | tf_op jit(solution)/shard_map/all_gather | solution.py:54
  25.5 422.8 %reduce-scatter.29.cloned.1.call-start = ((), (), s32[]{:S(2)}) async-start(), calls=%async_computation.21 | async-start | bytes 1310720 | tf_op jit(solution)/shard_map/reduce_scatter | solution.py:58
  51.2 18.5 %copy-start.9 = (bf16[16,128,128]{2,1,0:T(8,128)(2,1)}, bf16[16,128,128]{2,1,0:T(8,128)(2,1)S(1)}, u32[]{:S(2)}) copy-start(bf16[16,128,128]{2,1,0:T(8,128)(2,1)S(1)} %fusion.28) | copy-start | bytes 1572868
  51.2 18.7 %copy-start.21 = (bf16[128,2,2,4,128]{4,0,3,2,1:T(8,128)(2,1)}, bf16[128,2,2,4,128]{4,0,3,2,1:T(8,128)(2,1)S(1)}, u32[]{:S(2)}) copy-start(bf16[128,2,2,4,128]{4,0,3,2,1:T(8,128)(2,1)S(1)} %rev.54) | copy-start | bytes 1572868
  70.0 36.5 %copy-start.7 = (bf16[16,128,128]{2,1,0:T(8,128)(2,1)}, bf16[16,128,128]{2,1,0:T(8,128)(2,1)S(1)}, u32[]{:S(2)}) copy-start(bf16[16,128,128]{2,1,0:T(8,128)(2,1)S(1)} %fusion.29) | copy-start | bytes 1572868
  70.0 39.5 %copy-start.20 = (bf16[128,1,2,8,128]{4,0,3,2,1:T(8,128)(2,1)}, bf16[128,1,2,8,128]{4,0,3,2,1:T(8,128)(2,1)S(1)}, u32[]{:S(2)}) copy-start(bf16[128,1,2,8,128]{4,0,3,2,1:T(8,128)(2,1)S(1)} %rev.55) | copy-start | bytes 1572868
  106.5 26.9 %copy-start.5 = (bf16[1,16,2,128,128]{3,4,1,2,0:T(8,128)(2,1)}, bf16[1,16,2,128,128]{3,4,1,2,0:T(8,128)(2,1)S(1)}, u32[]{:S(2)}) copy-start(bf16[1,16,2,128,128]{3,4,1,2,0:T(8,128)(2,1)S(1)} %copy.133) | copy-start | bytes 3145732
  107.1 26.4 %collective-permute-start.6 = (bf16[128,16,128]{0,2,1:T(8,128)(2,1)S(1)}, bf16[128,16,128]{0,2,1:T(8,128)(2,1)}, u32[]{:S(2)}, u32[]{:S(2)}) collective-permute-start(bf16[128,16,128]{0,2,1:T(8,128)(2,1)S(1)} %fusion.59), channel_id=1, source_target_pairs={{0,4},{1,5},{2,6},{3,7},{4,0},{5,1},{6,2},{7,3},{8,12},{9,13},{10,... | collective-permute-start | bytes 1572872 | tf_op jit(solution)/shard_map/ppermute | solution.py:12
  110.9 24.1 %copy-start.31 = (bf16[128,16,128]{2,0,1:T(8,128)(2,1)}, bf16[128,16,128]{2,0,1:T(8,128)(2,1)S(1)}, u32[]{:S(2)}) copy-start(bf16[128,16,128]{2,0,1:T(8,128)(2,1)S(1)} %fusion.58) | copy-start | bytes 1572868
  110.9 33.4 %collective-permute-start = (bf16[128,16,128]{2,0,1:T(8,128)(2,1)S(1)}, bf16[128,16,128]{2,0,1:T(8,128)(2,1)S(1)}, u32[]{:S(2)}, u32[]{:S(2)}) collective-permute-start(bf16[128,16,128]{2,0,1:T(8,128)(2,1)S(1)} %fusion.58), channel_id=1, source_target_pairs={{0,1},{1,0},{2,3},{3,2},{4,5},{5,4},{6,7},{7,6},{8,9},{9,8},{10,11... | collective-permute-start | bytes 1572872 | tf_op jit(solution)/shard_map/ppermute | solution.py:12
  142.7 19.6 %collective-permute-start.7 = (bf16[128,16,128]{2,0,1:T(8,128)(2,1)S(1)}, bf16[128,16,128]{2,0,1:T(8,128)(2,1)}, u32[]{:S(2)}, u32[]{:S(2)}) collective-permute-start(bf16[128,16,128]{2,0,1:T(8,128)(2,1)S(1)} %fusion.60), channel_id=1, source_target_pairs={{0,2},{1,3},{2,0},{3,1},{4,6},{5,7},{6,4},{7,5},{8,10},{9,11},{10,... | collective-permute-start | bytes 1572872 | tf_op jit(solution)/shard_map/ppermute | solution.py:12
  145.8 36.4 %collective-permute-start.1 = (bf16[128,16,128]{2,0,1:T(8,128)(2,1)S(1)}, bf16[128,16,128]{2,0,1:T(8,128)(2,1)S(1)}, u32[]{:S(2)}, u32[]{:S(2)}) collective-permute-start(bf16[128,16,128]{2,0,1:T(8,128)(2,1)S(1)} %fusion.57), channel_id=1, source_target_pairs={{0,2},{1,3},{2,0},{3,1},{4,6},{5,7},{6,4},{7,5},{8,10},{9,11},{10,... | collective-permute-start | bytes 1572872 | tf_op jit(solution)/shard_map/ppermute | solution.py:12
  180.7 18.1 %collective-permute-start.8 = (bf16[128,16,128]{2,0,1:T(8,128)(2,1)}, bf16[128,16,128]{2,0,1:T(8,128)(2,1)}, u32[]{:S(2)}, u32[]{:S(2)}) collective-permute-start(bf16[128,16,128]{2,0,1:T(8,128)(2,1)} %fusion.61), channel_id=1, source_target_pairs={{0,1},{1,0},{2,3},{3,2},{4,5},{5,4},{6,7},{7,6},{8,9},{9,8},{10,11... | collective-permute-start | bytes 1572872 | tf_op jit(solution)/shard_map/ppermute | solution.py:12
  183.7 33.4 %collective-permute-start.2 = (bf16[128,16,128]{2,0,1:T(8,128)(2,1)S(1)}, bf16[128,16,128]{2,0,1:T(8,128)(2,1)}, u32[]{:S(2)}, u32[]{:S(2)}) collective-permute-start(bf16[128,16,128]{2,0,1:T(8,128)(2,1)S(1)} %fusion.56), channel_id=1, source_target_pairs={{0,4},{1,5},{2,6},{3,7},{4,0},{5,1},{6,2},{7,3},{8,12},{9,13},{10,... | collective-permute-start | bytes 1572872 | tf_op jit(solution)/shard_map/ppermute | solution.py:12
  262.5 186.9 %reduce-scatter.31.cloned.1.call-start = ((), (), s32[]{:S(2)}) async-start(), calls=%async_computation.22 | async-start | bytes 1310720 | tf_op jit(solution)/shard_map/reduce_scatter | solution.py:58
  280.1 170.4 %reduce-scatter.33.cloned.1.call-start = ((), (), s32[]{:S(2)}) async-start(), calls=%async_computation.23 | async-start | bytes 1310720 | tf_op jit(solution)/shard_map/reduce_scatter | solution.py:58
  288.3 163.3 %reduce-scatter.35.cloned.1.call-start = ((), (), s32[]{:S(2)}) async-start(), calls=%async_computation.24 | async-start | bytes 1310720 | tf_op jit(solution)/shard_map/reduce_scatter | solution.py:58
  296.1 156.6 %reduce-scatter.37.cloned.1.call-start = ((), (), s32[]{:S(2)}) async-start(), calls=%async_computation.25 | async-start | bytes 1310720 | tf_op jit(solution)/shard_map/reduce_scatter | solution.py:58
  302.2 14.1 %collective-permute-start.3 = (bf16[128,16,128]{2,0,1:T(8,128)(2,1)S(1)}, bf16[128,16,128]{2,0,1:T(8,128)(2,1)S(1)}, u32[]{:S(2)}, u32[]{:S(2)}) collective-permute-start(bf16[128,16,128]{2,0,1:T(8,128)(2,1)S(1)} %fusion.55), channel_id=1, source_target_pairs={{0,1},{1,0},{2,3},{3,2},{4,5},{5,4},{6,7},{7,6},{8,9},{9,8},{10,11... | collective-permute-start | bytes 1572872 | tf_op jit(solution)/shard_map/ppermute | solution.py:12
  305.2 26.4 %copy-start.16 = (bf16[128,16,128]{2,0,1:T(8,128)(2,1)}, bf16[128,16,128]{2,0,1:T(8,128)(2,1)S(1)}, u32[]{:S(2)}) copy-start(bf16[128,16,128]{2,0,1:T(8,128)(2,1)S(1)} %fusion.70) | copy-start | bytes 1572868
  305.6 26.0 %collective-permute-start.9 = (bf16[128,16,128]{2,0,1:T(8,128)(2,1)S(1)}, bf16[128,16,128]{2,0,1:T(8,128)(2,1)}, u32[]{:S(2)}, u32[]{:S(2)}) collective-permute-start(bf16[128,16,128]{2,0,1:T(8,128)(2,1)S(1)} %fusion.62), channel_id=1, source_target_pairs={{0,4},{1,5},{2,6},{3,7},{4,0},{5,1},{6,2},{7,3},{8,12},{9,13},{10,... | collective-permute-start | bytes 1572872 | tf_op jit(solution)/shard_map/ppermute | solution.py:12
  321.5 132.3 %reduce-scatter.39.cloned.1.call-start = ((), (), s32[]{:S(2)}) async-start(), calls=%async_computation.26 | async-start | bytes 1310720 | tf_op jit(solution)/shard_map/reduce_scatter | solution.py:58
  334.9 14.9 %collective-permute-start.10 = (bf16[128,16,128]{2,0,1:T(8,128)(2,1)S(1)}, bf16[128,16,128]{2,0,1:T(8,128)(2,1)S(1)}, u32[]{:S(2)}, u32[]{:S(2)}) collective-permute-start(bf16[128,16,128]{2,0,1:T(8,128)(2,1)S(1)} %fusion.63), channel_id=1, source_target_pairs={{0,2},{1,3},{2,0},{3,1},{4,6},{5,7},{6,4},{7,5},{8,10},{9,11},{10,... | collective-permute-start | bytes 1572872 | tf_op jit(solution)/shard_map/ppermute | solution.py:12
  336.0 23.2 %collective-permute-start.4 = (bf16[128,16,128]{2,0,1:T(8,128)(2,1)S(1)}, bf16[128,16,128]{2,0,1:T(8,128)(2,1)S(1)}, u32[]{:S(2)}, u32[]{:S(2)}) collective-permute-start(bf16[128,16,128]{2,0,1:T(8,128)(2,1)S(1)} %fusion.54), channel_id=1, source_target_pairs={{0,2},{1,3},{2,0},{3,1},{4,6},{5,7},{6,4},{7,5},{8,10},{9,11},{10,... | collective-permute-start | bytes 1572872 | tf_op jit(solution)/shard_map/ppermute | solution.py:12
  351.6 10.6 %collective-permute-start.11 = (bf16[128,16,128]{2,0,1:T(8,128)(2,1)}, bf16[128,16,128]{2,0,1:T(8,128)(2,1)}, u32[]{:S(2)}, u32[]{:S(2)}) collective-permute-start(bf16[128,16,128]{2,0,1:T(8,128)(2,1)} %fusion.64), channel_id=1, source_target_pairs={{0,1},{1,0},{2,3},{3,2},{4,5},{5,4},{6,7},{7,6},{8,9},{9,8},{10,11... | collective-permute-start | bytes 1572872 | tf_op jit(solution)/shard_map/ppermute | solution.py:12
  362.2 99.2 %reduce-scatter.15.cloned.1.call-start = ((), (), s32[]{:S(2)}) async-start(), calls=%async_computation.14 | async-start | bytes 1310720 | tf_op jit(solution)/shard_map/reduce_scatter | solution.py:58
  381.2 107.9 %reduce-scatter.17.cloned.1.call-start = ((), (), s32[]{:S(2)}) async-start(), calls=%async_computation.15 | async-start | bytes 1310720 | tf_op jit(solution)/shard_map/reduce_scatter | solution.py:58
  387.5 128.9 %reduce-scatter.19.cloned.1.call-start = ((), (), s32[]{:S(2)}) async-start(), calls=%async_computation.16 | async-start | bytes 1310720 | tf_op jit(solution)/shard_map/reduce_scatter | solution.py:58
  393.4 150.6 %reduce-scatter.21.cloned.1.call-start = ((), (), s32[]{:S(2)}) async-start(), calls=%async_computation.17 | async-start | bytes 1310720 | tf_op jit(solution)/shard_map/reduce_scatter | solution.py:58
  399.3 172.1 %reduce-scatter.23.cloned.1.call-start = ((), (), s32[]{:S(2)}) async-start(), calls=%async_computation.18 | async-start | bytes 1310720 | tf_op jit(solution)/shard_map/reduce_scatter | solution.py:58
  402.7 196.2 %reduce-scatter.25.cloned.1.call-start = ((), (), s32[]{:S(2)}) async-start(), calls=%async_computation.19 | async-start | bytes 1310720 | tf_op jit(solution)/shard_map/reduce_scatter | solution.py:58
  406.2 220.0 %reduce-scatter.27.cloned.1.call-start = ((), (), s32[]{:S(2)}) async-start(), calls=%async_computation.20 | async-start | bytes 1310720 | tf_op jit(solution)/shard_map/reduce_scatter | solution.py:58
  410.0 243.8 %reduce-scatter.41.cloned.1.call-start = ((), (), s32[]{:S(2)}) async-start(), calls=%async_computation.27 | async-start | bytes 1310720 | tf_op jit(solution)/shard_map/reduce_scatter | solution.py:58
  413.7 26.5 %collective-permute-start.5 = (bf16[128,16,128]{2,0,1:T(8,128)(2,1)}, bf16[128,16,128]{2,0,1:T(8,128)(2,1)}, u32[]{:S(2)}, u32[]{:S(2)}) collective-permute-start(bf16[128,16,128]{2,0,1:T(8,128)(2,1)} %fusion.53), channel_id=1, source_target_pairs={{0,4},{1,5},{2,6},{3,7},{4,0},{5,1},{6,2},{7,3},{8,12},{9,13},{10,... | collective-permute-start | bytes 1572872 | tf_op jit(solution)/shard_map/ppermute | solution.py:12
  (67 other events, 334.4 us)
Sparse Core Ops, SparseCore 0:
  11.0 19.4 all-gather.28
  32.5 16.7 all-gather.30
  51.4 16.7 all-gather.32
  69.6 16.7 all-gather.34
  87.8 16.7 all-gather.54
  106.0 16.7 all-gather.36
  124.3 16.7 all-gather.52
  143.2 16.7 all-gather.38
  161.5 16.7 all-gather.50
  179.7 16.7 all-gather.40
  198.0 16.7 all-gather.48
  216.2 16.7 all-gather.46
  234.5 16.7 all-gather.44
  252.7 16.7 all-gather.42
  271.8 24.8 reduce-scatter.28
  299.3 24.8 reduce-scatter.30
  326.6 24.9 reduce-scatter.32
  354.1 24.8 reduce-scatter.34
  381.6 24.8 reduce-scatter.36
  409.0 24.8 reduce-scatter.38
  436.5 24.8 reduce-scatter.14
  464.1 24.8 reduce-scatter.16
  491.6 24.8 reduce-scatter.18
  519.0 24.9 reduce-scatter.20
  546.5 24.8 reduce-scatter.22
  573.9 24.9 reduce-scatter.24
  601.3 24.8 reduce-scatter.26
  628.9 24.9 reduce-scatter.40
where the time goes:
time: 670 us; the launch traced here: 664 us
  waiting for transfers between devices  402 us (60%)
  local copies, waits for them, and re-layouts  104 us (16%)
  matrix products  99.5 us (15%)
  starting transfers between devices  22.8 us (3%)
  other arithmetic  20.2 us (3%)
  between operations  15.9 us (2%)
    reduce_scatter x14, waiting for transfers between devices, sum_level(): lax.psum_scatter(level_grad.astype(jnp.bfloat16), 'dp', scatter_dimension...  183 us
    all_gather x14, waiting for transfers between devices, gather_level(): return lax.all_gather(factor_shard, 'dp', axis=2, tiled=True)  166 us
    ppermute x12, waiting for transfers between devices, partner_2(): return lax.ppermute(value, axis, pairs)  52.8 us
    unnamed x178, local copies, waits for them, and re-layouts  39.1 us
    convert_element_type x14, local copies, waits for them, and re-layouts, sum_level(): level_grad.astype(jnp.bfloat16)  34.1 us
    dot_general x14, matrix products, apply_level(): jnp.einsum('tjr,jrc->tjc', values, factor[:, 0], preferred_element_type=j...  22.7 us
    dot_general x14, matrix products, backward_map(): jnp.einsum('tjc,jrc->tjr', current, factor[:, 0], preferred_element_type=...  21.4 us
    ppermute x12, starting transfers between devices, partner_2(): return lax.ppermute(value, axis, pairs)  20.8 us
  transfers between devices with their start and end apart: 40, of which 28 were waited for; matrix products, arithmetic and copies ran while one was open for 32% of the time, Pallas kernels for 0%

commit v1 on v0

--- a/solution.py
+++ b/solution.py
@@ -1,8 +1,11 @@
+import functools
 import math
 
 import jax
 import jax.numpy as jnp
 from jax import lax
+from jax.experimental import pallas as pl
+from jax.experimental.pallas import tpu as pltpu
 from jax.sharding import PartitionSpec as P
 
 
@@ -126,6 +129,303 @@
     )
 
 
+def block_of(values, j, width):
+    return values[:, j * width:(j + 1) * width]
+
+
+def start_factor_copies(pieces, factor_buf, sems, levels):
+    me = lax.axis_index("dp")
+    rows = pieces[0].shape[3]
+    copies = []
+    for slot, level in enumerate(levels):
+        row = []
+        for k, piece in enumerate(pieces):
+            at = pl.multiple_of((me ^ k) * rows, rows)
+            copy = pltpu.make_async_copy(
+                piece.at[level],
+                factor_buf.at[slot, :, :, pl.ds(at, rows), :],
+                sems.at[slot, k],
+            )
+            copy.start()
+            row.append(copy)
+        copies.append(row)
+    return copies
+
+
+def merged(factor_buf, slot, j):
+    both = factor_buf[slot, j]
+    return both.reshape(both.shape[0] * both.shape[1], both.shape[2])
+
+
+def forward_kernel(levels, bits, partner_given, *refs):
+    n = len(levels)
+    values = refs[0]
+    partner = refs[1] if partner_given else None
+    base = 2 if partner_given else 1
+    pieces = refs[base:base + 4]
+    outs = refs[base + 4:base + 4 + n]
+    factor_buf, sems = refs[base + 4 + n:]
+    width = factor_buf.shape[3]
+    count = factor_buf.shape[1]
+    copies = start_factor_copies(pieces, factor_buf, sems, levels)
+    for slot in range(n):
+        for copy in copies[slot]:
+            copy.wait()
+        for j in range(count):
+            if partner_given:
+                other = block_of(partner, j, width)
+            else:
+                other = block_of(values, j ^ (1 << bits[slot]), width)
+            pair = jnp.concatenate([block_of(values, j, width), other], axis=1)
+            got = jnp.dot(pair, merged(factor_buf, slot, j), preferred_element_type=jnp.float32)
+            outs[slot][:, j * width:(j + 1) * width] = got.astype(outs[slot].dtype)
+        values = outs[slot]
+
+
+def backward_kernel(levels, bits, remote, summed, *refs):
+    n = len(levels)
+    base = 2 if summed else 1
+    pieces = refs[base:base + 4]
+    n_out = (2 if remote else n) + (1 if summed else 0)
+    outs = list(refs[base + 4:base + 4 + n_out])
+    factor_buf, sems = refs[base + 4 + n_out:base + 6 + n_out]
+    width = factor_buf.shape[3]
+    count = factor_buf.shape[1]
+    copies = start_factor_copies(pieces, factor_buf, sems, levels)
+    current = refs[0]
+    if summed:
+        first = outs.pop(0)
+        first[...] = (refs[0][...] + refs[1][...].astype(jnp.float32)).astype(first.dtype)
+        current = first
+    for slot in range(n):
+        for copy in copies[slot]:
+            copy.wait()
+
+        def through(j):
+            got = lax.dot_general(
+                block_of(current, j, width),
+                merged(factor_buf, slot, j),
+                (((1,), (1,)), ((), ())),
+                preferred_element_type=jnp.float32,
+            )
+            return got[:, :width], got[:, width:].astype(jnp.bfloat16)
+
+        for j in range(count):
+            if remote:
+                own, other = through(j)
+                outs[0][:, j * width:(j + 1) * width] = own
+                outs[1][:, j * width:(j + 1) * width] = other
+            else:
+                p = j ^ (1 << bits[slot])
+                if p < j:
+                    continue
+                own_j, other_j = through(j)
+                own_p, other_p = through(p)
+                dst = outs[slot]
+                dst[:, j * width:(j + 1) * width] = (
+                    own_j + other_p.astype(jnp.float32)
+                ).astype(dst.dtype)
+                dst[:, p * width:(p + 1) * width] = (
+                    own_p + other_j.astype(jnp.float32)
+                ).astype(dst.dtype)
+        if not remote:
+            current = outs[slot]
+
+
+def grad_kernel(bits, remote, grad_scale, *refs):
+    n = len(bits)
+    values = refs[:n]
+    partners = refs[n:2 * n] if remote else None
+    base = 2 * n if remote else n
+    grads = refs[base:base + n]
+    keep, send = refs[base + n:]
+    count = keep.shape[2]
+    rows = keep.shape[4]
+    width = keep.shape[5]
+    me = lax.axis_index("dp")
+    core = me % 2
+    x_at = me // 2
+    for slot in range(n):
+        for j in range(count):
+            if remote:
+                other = block_of(partners[slot], j, width)
+            else:
+                other = block_of(values[slot], j ^ (1 << bits[slot]), width)
+            pair = jnp.concatenate([block_of(values[slot], j, width), other], axis=1)
+            got = lax.dot_general(
+                pair,
+                block_of(grads[slot], j, width),
+                (((0,), (0,)), ((), ())),
+                preferred_element_type=jnp.float32,
+            ) * grad_scale
+            for term in range(2):
+                for x_to in range(2):
+                    at = term * width + x_to * 2 * rows
+                    low = got[at:at + rows]
+                    high = got[at + rows:at + 2 * rows]
+                    k_x = x_at ^ x_to
+                    keep[k_x, slot, j, term] = jnp.where(core == 0, low, high).astype(keep.dtype)
+                    send[k_x, slot, j, term] = jnp.where(core == 0, high, low).astype(send.dtype)
+
+
+VMEM = pl.BlockSpec(memory_space=pltpu.VMEM)
+ANY = pl.BlockSpec(memory_space=pl.ANY)
+PARAMS = dict(compiler_params=pltpu.CompilerParams(vmem_limit_bytes=40 * 2**20))
+
+
+def estimate(n_levels, tok_rows, count, width, moved):
+    return pl.CostEstimate(
+        flops=4 * n_levels * tok_rows * count * width * width,
+        bytes_accessed=moved,
+        transcendentals=0,
+    )
+
+
+def call_forward(values, partner, pieces, levels, bits, out_type=jnp.bfloat16):
+    n = len(levels)
+    _, count, two, rows, width = pieces[0].shape
+    acts = [values] if partner is None else [values, partner]
+    buf = (n, count, two, 4 * rows, width)
+    return pl.pallas_call(
+        functools.partial(forward_kernel, levels, bits, partner is not None),
+        out_shape=[jax.ShapeDtypeStruct(values.shape, out_type)] * n,
+        in_specs=[VMEM] * len(acts) + [ANY] * 4,
+        out_specs=[VMEM] * n,
+        scratch_shapes=[pltpu.VMEM(buf, jnp.bfloat16), pltpu.SemaphoreType.DMA((n, 4))],
+        cost_estimate=estimate(n, values.shape[0], count, width, 2 * math.prod(buf) + 4 * n * values.size),
+        **PARAMS,
+    )(*acts, *pieces)
+
+
+def call_backward(incoming, pieces, levels, bits, remote):
+    n = len(levels)
+    _, count, two, rows, width = pieces[0].shape
+    buf = (n, count, two, 4 * rows, width)
+    shape = incoming[0].shape
+    low = jax.ShapeDtypeStruct(shape, jnp.bfloat16)
+    outs = [low] if len(incoming) == 2 else []
+    outs += [jax.ShapeDtypeStruct(shape, jnp.float32), low] if remote else [low] * n
+    return pl.pallas_call(
+        functools.partial(backward_kernel, levels, bits, remote, len(incoming) == 2),
+        out_shape=outs,
+        in_specs=[VMEM] * len(incoming) + [ANY] * 4,
+        out_specs=[VMEM] * len(outs),
+        scratch_shapes=[pltpu.VMEM(buf, jnp.bfloat16), pltpu.SemaphoreType.DMA((n, 4))],
+        cost_estimate=estimate(n, shape[0], count, width, 2 * math.prod(buf) + 6 * n * math.prod(shape)),
+        **PARAMS,
+    )(*incoming, *pieces)
+
+
+def call_grads(values, partners, grads, bits, rows, grad_scale):
+    n = len(bits)
+    tok_rows, features = values[0].shape
+    width = 4 * rows
+    count = features // width
+    out = jax.ShapeDtypeStruct((2, n, count, 2, rows, width), jnp.bfloat16)
+    acts = list(values) + list(partners or []) + list(grads)
+    return pl.pallas_call(
+        functools.partial(grad_kernel, bits, partners is not None, grad_scale),
+        out_shape=[out, out],
+        in_specs=[VMEM] * len(acts),
+        out_specs=[VMEM] * 2,
+        cost_estimate=estimate(n, tok_rows, count, width, 10 * n * values[0].size),
+        **PARAMS,
+    )(*acts)
+
+
+def sum_pairs(keep, send):
+    got = partner_dp(send, 1)
+    across = (keep[1].astype(jnp.float32) + got[1].astype(jnp.float32)).astype(jnp.bfloat16)
+    mine = keep[0].astype(jnp.float32) + got[0].astype(jnp.float32)
+    return mine + partner_dp(across, 2).astype(jnp.float32)
+
+
+def partner_dp(value, mask):
+    return lax.ppermute(value, "dp", [(k, k ^ mask) for k in range(lax.axis_size("dp"))])
+
+
+def gather_pairs(shard):
+    near = partner_dp(shard, 1)
+    far = partner_dp(shard, 2)
+    return [shard, near, far, partner_dp(far, 1)]
+
+
+def on_device_pairs(tokens, cotangent, factor_in, factor_out):
+    level_count, local_blocks, _, rows, width = factor_in.shape
+    local_bits = local_blocks.bit_length() - 1
+    grad_scale = 1.0 / math.sqrt(tokens.shape[0] * lax.axis_size("dp"))
+    low = tuple(range(local_bits))
+    high = tuple(range(local_bits, level_count))
+
+    in_low = gather_pairs(factor_in[:local_bits])
+    in_high = gather_pairs(factor_in[local_bits:])
+    out_high = gather_pairs(factor_out[local_bits:])
+    out_low = gather_pairs(factor_out[:local_bits])
+
+    def over_feat(value, level):
+        return partner_2(value, "feat", level - local_bits)
+
+    def forward(values, pieces_low, pieces_high, last_type):
+        stored = [values] + list(call_forward(values, None, pieces_low, low, low))
+        partners = []
+        for level in high:
+            partner = over_feat(stored[level], level)
+            partners.append(partner)
+            out_type = last_type if level == level_count - 1 else jnp.bfloat16
+            stored += call_forward(
+                stored[level], partner, pieces_high, (level - local_bits,), (level,), out_type
+            )
+        return stored, partners
+
+    def backward(grad, pieces_low, pieces_high):
+        grads = [None] * level_count
+        incoming = [grad]
+        for level in reversed(high):
+            *head, own, other = call_backward(
+                incoming, pieces_high, (level - local_bits,), (level,), True
+            )
+            if level == level_count - 1:
+                grads[level] = grad
+            else:
+                grads[level] = head[0]
+            incoming = [own, over_feat(other, level)]
+        down = tuple(reversed(low))
+        got = call_backward(incoming, pieces_low, down, down, False)
+        for place, level in enumerate(down):
+            grads[level] = got[place]
+        return got[-1], grads
+
+    def level_sums(stored, partners, grads, group):
+        remote = group[0] >= local_bits
+        keep, send = call_grads(
+            [stored[level] for level in group],
+            [partners[level - local_bits] for level in group] if remote else None,
+            [grads[level] for level in group],
+            group,
+            rows,
+            grad_scale,
+        )
+        return sum_pairs(keep, send)
+
+    stored_in, partners_in = forward(tokens, in_low, in_high, jnp.float32)
+    grad_mid, grads_out = backward(cotangent, out_low, out_high)
+    pre_gelu = stored_in[-1]
+    hidden = gelu_exact(pre_gelu).astype(jnp.bfloat16)
+    grad_pre = (grad_mid.astype(jnp.float32) * gelu_slope(pre_gelu)).astype(jnp.bfloat16)
+    stored_out, partners_out = forward(hidden, out_low, out_high, jnp.bfloat16)
+    token_grad, grads_in = backward(grad_pre, in_low, in_high)
+    half = local_bits // 2
+    groups = [low[:half], low[half:], high]
+    sums_out = [level_sums(stored_out, partners_out, grads_out, group) for group in groups]
+    sums_in = [level_sums(stored_in, partners_in, grads_in, group) for group in reversed(groups)]
+    return (
+        stored_out[-1],
+        token_grad,
+        jnp.concatenate(sums_in[::-1], 0),
+        jnp.concatenate(sums_out, 0),
+    )
+
+
 def solution(mesh):
     placed = (
         P("dp", "feat"),
@@ -133,8 +433,9 @@
         P(None, "feat", None, "dp", None),
         P(None, "feat", None, "dp", None),
     )
+    pairs = mesh.shape["dp"] == 4
     return jax.shard_map(
-        on_device,
+        on_device_pairs if pairs else on_device,
         mesh=mesh,
         in_specs=placed,
         out_specs=(

time: 670 us -> 288 us (0.43)
  waiting for transfers between devices: 402 us -> 198 us
  matrix products: 99.5 us -> 0 us
  local copies, waits for them, and re-layouts: 104 us -> 9.63 us
  Pallas kernels: 0 us -> 25.5 us
  between operations: 15.9 us -> 1.28 us
  starting transfers between devices: 22.8 us -> 34.8 us
    reduce_scatter x14 -> x0, waiting for transfers between devices: 183 us -> none  [sum_level(): lax.psum_scatter(level_grad.astype(jnp.bfloat16), 'dp', scatter_dimension...]
    all_gather x14 -> x0, waiting for transfers between devices: 166 us -> none  [gather_level(): return lax.all_gather(factor_shard, 'dp', axis=2, tiled=True)]
    dot_general x84 -> x0, matrix products: 99.5 us -> none  [the longest x14 22.7 us: apply_level(): jnp.einsum('tjr,jrc->tjc', values, factor[:, 0], preferred_element_type=j...]
    ppermute x0 -> x24, waiting for transfers between devices: none -> 97.1 us  [partner_dp(): lax.ppermute(value, 'dp', [(k, k ^ mask) for k in range(lax.axis_size('dp...]
    ppermute x12, waiting for transfers between devices: 52.8 us -> 101 us  [partner_2(): return lax.ppermute(value, axis, pairs)]
    convert_element_type x14 -> x0, local copies, waits for them, and re-layouts: 34.1 us -> none  [sum_level(): level_grad.astype(jnp.bfloat16)]
    unnamed x178 -> x72, local copies, waits for them, and re-layouts: 39.1 us -> 6.89 us
    pallas_call x0 -> x22, Pallas kernels: none -> 25.5 us  [the longest x8 9.4 us: call_backward(): pl.pallas_call(functools.partial(backward_kernel, levels, bits, remote, l...]
  transfers between devices with their start and end apart: 40 -> 36, of which waited for: 28 -> 15; matrix products, arithmetic and copies ran while one was open for 32% -> 6% of each run, Pallas kernels for 0% -> 8%
where the time goes in v1:
time: 288 us; the launch traced here: 287 us
  waiting for transfers between devices  198 us (69%)
  starting transfers between devices  34.8 us (12%)
  Pallas kernels  25.5 us (9%)
  other arithmetic  18.3 us (6%)
  local copies, waits for them, and re-layouts  9.63 us (3%)
    ppermute x12, waiting for transfers between devices, partner_2(): return lax.ppermute(value, axis, pairs)  101 us
    ppermute x24, waiting for transfers between devices, partner_dp(): lax.ppermute(value, 'dp', [(k, k ^ mask) for k in range(lax.axis_size('dp...  97.1 us
    ppermute x12, starting transfers between devices, partner_2(): return lax.ppermute(value, axis, pairs)  18.1 us
    ppermute x24, starting transfers between devices, partner_dp(): lax.ppermute(value, 'dp', [(k, k ^ mask) for k in range(lax.axis_size('dp...  16.8 us
    pallas_call x8, Pallas kernels, call_backward(): pl.pallas_call(functools.partial(backward_kernel, levels, bits, remote, l...  9.4 us
    pallas_call x8, Pallas kernels, call_forward(): pl.pallas_call(functools.partial(forward_kernel, levels, bits, partner is...  8.59 us
    pallas_call x6, Pallas kernels, call_grads(): pl.pallas_call(functools.partial(grad_kernel, bits, partners is not None,...  7.49 us
    unnamed x72, local copies, waits for them, and re-layouts  6.89 us
  transfers between devices with their start and end apart: 36, of which 15 were waited for; matrix products, arithmetic and copies ran while one was open for 6% of the time, Pallas kernels for 8%

profile of v1, /device:TPU:0, one launch (start us, length us, event | category | flops | bytes accessed | tf_op | source)
XLA Modules:
  0.0 287.2 jit_solution(11211073861290050349)
XLA Ops:
  0.6 1.4 slice.84.refs_1_.refs_2_
  2.1 3.0 %collective-permute-start.1 = (bf16[4,16,2,32,128]{4,3,2,1,0:T(8,128)(2,1)S(1)}, bf16[4,16,2,32,128]{4,3,2,1,0:T(8,128)(2,1)S(1)}, u32[]{:S(2)}, u32[]{:S(2)}) collective-permute-start(bf16[4,16,2,32,128]{4,3,2,1,0:T(8,128)(2,1)S(1)} %slice.84.refs_1_.refs_2_), channel_id=1, source_target_pairs={{0,16},{8,24},{16,0},{24,8},{1,17},{9,25},{17,1},{25,9},{2,18},{10... | collective-permute-start | bytes 3145736 | tf_op jit(solution)/shard_map/ppermute | solution.py:344
  6.0 23.0 %collective-permute-done.1.refs_3_.refs_4_ = bf16[4,16,2,32,128]{4,3,2,1,0:T(8,128)(2,1)S(1)} collective-permute-done((bf16[4,16,2,32,128]{4,3,2,1,0:T(8,128)(2,1)S(1)}, bf16[4,16,2,32,128]{4,3,2,1,0:T(8,128)(2,1)S(1)}, u32[]{:S(2)}, u32[]{:S(2)}) %collective-permute-start.1) | collective-permute-done | bytes 1048608 | tf_op jit(solution)/shard_map/ppermute | solution.py:344
  30.3 2.1 collective-permute-start.5
  32.4 13.5 %collective-permute-done.14.refs_4_.refs_3_ = bf16[3,16,2,32,128]{4,3,2,1,0:T(8,128)(2,1)S(1)} collective-permute-done((bf16[3,16,2,32,128]{4,3,2,1,0:T(8,128)(2,1)S(1)}, bf16[3,16,2,32,128]{4,3,2,1,0:T(8,128)(2,1)S(1)}, u32[]{:S(2)}, u32[]{:S(2)}) %collective-permute-start.14) | collective-permute-done | bytes 786464 | tf_op jit(solution)/shard_map/ppermute | solution.py:344
  46.0 2.1 collective-permute-start.10
  48.1 14.6 %collective-permute-done.5.refs_4_.refs_3_ = bf16[3,16,2,32,128]{4,3,2,1,0:T(8,128)(2,1)S(1)} collective-permute-done((bf16[3,16,2,32,128]{4,3,2,1,0:T(8,128)(2,1)S(1)}, bf16[3,16,2,32,128]{4,3,2,1,0:T(8,128)(2,1)S(1)}, u32[]{:S(2)}, u32[]{:S(2)}) %collective-permute-start.5) | collective-permute-done | bytes 786464 | tf_op jit(solution)/shard_map/ppermute | solution.py:344
  63.9 3.2 %collective-permute-start.18 = (bf16[128,2048]{1,0:T(8,128)(2,1)S(1)}, bf16[128,2048]{1,0:T(8,128)(2,1)S(1)}, u32[]{:S(2)}, u32[]{:S(2)}) collective-permute-start(bf16[128,2048]{1,0:T(8,128)(2,1)S(1)} %get-tuple-element.53), channel_id=1, source_target_pairs={{0,4},{1,5},{2,6},{3,7},{4,0},{5,1},{6,2},{7,3},{8,12},{9,13},{10,... | collective-permute-start | bytes 1572872 | tf_op jit(solution)/shard_map/ppermute | solution.py:15
  67.1 2.2 shard_map.75
  70.9 1.5 collective-permute-start.3
  72.4 18.0 %collective-permute-done.18.refs_1_ = bf16[128,2048]{1,0:T(8,128)(2,1)S(1)} collective-permute-done((bf16[128,2048]{1,0:T(8,128)(2,1)S(1)}, bf16[128,2048]{1,0:T(8,128)(2,1)S(1)}, u32[]{:S(2)}, u32[]{:S(2)}) %collective-permute-start.18) | collective-permute-done | bytes 524320 | tf_op jit(solution)/shard_map/ppermute | solution.py:15
  93.2 1.3 collective-permute-start.7
  94.5 11.5 %collective-permute-done.19.refs_1_ = bf16[128,2048]{1,0:T(8,128)(2,1)S(1)} collective-permute-done((bf16[128,2048]{1,0:T(8,128)(2,1)S(1)}, bf16[128,2048]{1,0:T(8,128)(2,1)S(1)}, u32[]{:S(2)}, u32[]{:S(2)}) %collective-permute-start.19) | collective-permute-done | bytes 524320 | tf_op jit(solution)/shard_map/ppermute | solution.py:15
  108.5 1.6 collective-permute-start.20
  110.0 5.7 %collective-permute-done.7.refs_1_.refs_4_ = bf16[128,2048]{1,0:T(8,128)(2,1)S(1)} collective-permute-done((bf16[128,2048]{1,0:T(8,128)(2,1)S(1)}, bf16[128,2048]{1,0:T(8,128)(2,1)S(1)}, u32[]{:S(2)}, u32[]{:S(2)}) %collective-permute-start.7) | collective-permute-done | bytes 524320 | tf_op jit(solution)/shard_map/ppermute | solution.py:15
  116.5 2.9 %collective-permute-start.8 = (bf16[128,2048]{1,0:T(8,128)(2,1)S(1)}, bf16[128,2048]{1,0:T(8,128)(2,1)S(1)}, u32[]{:S(2)}, u32[]{:S(2)}) collective-permute-start(bf16[128,2048]{1,0:T(8,128)(2,1)S(1)} %shard_map.77.refs_0_.refs_2_), channel_id=1, source_target_pairs={{0,4},{1,5},{2,6},{3,7},{4,0},{5,1},{6,2},{7,3},{8,12},{9,13},{10,... | collective-permute-start | bytes 1572872 | tf_op jit(solution)/shard_map/ppermute | solution.py:15
  119.4 2.3 shard_map.86
  121.8 20.4 %collective-permute-done.8.refs_1_.refs_5_ = bf16[128,2048]{1,0:T(8,128)(2,1)S(1)} collective-permute-done((bf16[128,2048]{1,0:T(8,128)(2,1)S(1)}, bf16[128,2048]{1,0:T(8,128)(2,1)S(1)}, u32[]{:S(2)}, u32[]{:S(2)}) %collective-permute-start.8) | collective-permute-done | bytes 524320 | tf_op jit(solution)/shard_map/ppermute | solution.py:15
  145.1 2.3 shard_map.79
  147.5 1.6 collective-permute-start.12
  150.0 20.2 %collective-permute-done.21.refs_1_ = bf16[128,2048]{1,0:T(8,128)(2,1)S(1)} collective-permute-done((bf16[128,2048]{1,0:T(8,128)(2,1)S(1)}, bf16[128,2048]{1,0:T(8,128)(2,1)S(1)}, u32[]{:S(2)}, u32[]{:S(2)}) %collective-permute-start.21) | collective-permute-done | bytes 524320 | tf_op jit(solution)/shard_map/ppermute | solution.py:15
  172.3 1.8 shard_map.94
  175.0 1.7 collective-permute-start.16
  176.8 9.0 %collective-permute-done.22.refs_1_ = bf16[128,2048]{1,0:T(8,128)(2,1)S(1)} collective-permute-done((bf16[128,2048]{1,0:T(8,128)(2,1)S(1)}, bf16[128,2048]{1,0:T(8,128)(2,1)S(1)}, u32[]{:S(2)}, u32[]{:S(2)}) %collective-permute-start.22) | collective-permute-done | bytes 524320 | tf_op jit(solution)/shard_map/ppermute | solution.py:15
  186.4 1.6 collective-permute-start.23
  188.0 6.2 %collective-permute-done.16.refs_1_.refs_4_ = bf16[128,2048]{1,0:T(8,128)(2,1)S(1)} collective-permute-done((bf16[128,2048]{1,0:T(8,128)(2,1)S(1)}, bf16[128,2048]{1,0:T(8,128)(2,1)S(1)}, u32[]{:S(2)}, u32[]{:S(2)}) %collective-permute-start.16) | collective-permute-done | bytes 524320 | tf_op jit(solution)/shard_map/ppermute | solution.py:15
  194.8 1.8 collective-permute-start.17
  196.7 2.0 fusion.11
  198.7 1.5 collective-permute-start.33
  200.2 2.2 shard_map.93
  202.5 3.3 %shard_map.90 = (bf16[128,2048]{1,0:T(8,128)(2,1)S(1)}, bf16[128,2048]{1,0:T(8,128)(2,1)S(1)}, bf16[128,2048]{1,0:T(8,128)(2,1)S(1)}, bf16[128,2048]{1,0:T(8,128)(2,1)S(1)}, bf16[128,2048]{1,0:T(8,128)(2,1)}) custom-call(f32[128,2048]{1,0:T(8,128)S(1)} %get-tuple-element.63.refs_0_, bf16[128,2048]{1,0:T(8,128)(2,1)S(1)} %collective-permute-done.23.refs_1_, ...), custom_call_target="tpu_custom_call" | custom-call | flops 536870912 | bytes 10485760 | tf_op jit(solution)/shard_map/pallas_call | solution.py:308
  207.3 1.3 fusion.10
  210.0 9.5 %collective-permute-done.17.refs_1_.refs_5_ = bf16[128,2048]{1,0:T(8,128)(2,1)S(1)} collective-permute-done((bf16[128,2048]{1,0:T(8,128)(2,1)S(1)}, bf16[128,2048]{1,0:T(8,128)(2,1)S(1)}, u32[]{:S(2)}, u32[]{:S(2)}) %collective-permute-start.17) | collective-permute-done | bytes 524320 | tf_op jit(solution)/shard_map/ppermute | solution.py:15
  221.2 1.3 shard_map.82
  222.5 1.5 bitcast_add_fusion.2
  224.0 1.3 bitcast_add_fusion.3
  225.5 1.6 collective-permute-start.27
  227.1 1.2 fusion.8
  228.9 1.5 fusion.6
  230.4 1.6 collective-permute-start.29
  232.9 7.5 %collective-permute-done.27 = bf16[2,16,2,32,128]{4,3,2,1,0:T(8,128)(2,1)S(1)} collective-permute-done((bf16[2,16,2,32,128]{4,3,2,1,0:T(8,128)(2,1)S(1)}, bf16[2,16,2,32,128]{4,3,2,1,0:T(8,128)(2,1)S(1)}, u32[]{:S(2)}, u32[]{:S(2)}) %collective-permute-start.27) | collective-permute-done | bytes 524320 | tf_op jit(solution)/shard_map/ppermute | solution.py:344
  240.7 11.0 %collective-permute-done.25 = bf16[2,16,2,32,128]{4,3,2,1,0:T(8,128)(2,1)S(1)} collective-permute-done((bf16[2,16,2,32,128]{4,3,2,1,0:T(8,128)(2,1)S(1)}, bf16[2,16,2,32,128]{4,3,2,1,0:T(8,128)(2,1)S(1)}, u32[]{:S(2)}, u32[]{:S(2)}) %collective-permute-start.25) | collective-permute-done | bytes 524320 | tf_op jit(solution)/shard_map/ppermute | solution.py:344
  251.6 1.3 bitcast_add_fusion.5
  252.9 15.5 %collective-permute-done.29 = bf16[3,16,2,32,128]{4,3,2,1,0:T(8,128)(2,1)S(1)} collective-permute-done((bf16[3,16,2,32,128]{4,3,2,1,0:T(8,128)(2,1)S(1)}, bf16[3,16,2,32,128]{4,3,2,1,0:T(8,128)(2,1)S(1)}, u32[]{:S(2)}, u32[]{:S(2)}) %collective-permute-start.29) | collective-permute-done | bytes 786464 | tf_op jit(solution)/shard_map/ppermute | solution.py:344
  268.5 1.6 bitcast_add_fusion.1
  270.0 2.5 pad_maximum_fusion
  272.6 11.8 %collective-permute-done.35 = bf16[3,16,2,32,128]{4,3,2,1,0:T(8,128)(2,1)S(1)} collective-permute-done((bf16[3,16,2,32,128]{4,3,2,1,0:T(8,128)(2,1)S(1)}, bf16[3,16,2,32,128]{4,3,2,1,0:T(8,128)(2,1)S(1)}, u32[]{:S(2)}, u32[]{:S(2)}) %collective-permute-start.35) | collective-permute-done | bytes 786464 | tf_op jit(solution)/shard_map/ppermute | solution.py:344
  284.8 2.4 pad_maximum_fusion.1
  (137 shorter events, 25.7 us)
Async XLA Ops:
  2.1 27.0 %collective-permute-start.1 = (bf16[4,16,2,32,128]{4,3,2,1,0:T(8,128)(2,1)S(1)}, bf16[4,16,2,32,128]{4,3,2,1,0:T(8,128)(2,1)S(1)}, u32[]{:S(2)}, u32[]{:S(2)}) collective-permute-start(bf16[4,16,2,32,128]{4,3,2,1,0:T(8,128)(2,1)S(1)} %slice.84.refs_1_.refs_2_), channel_id=1, source_target_pairs={{0,16},{8,24},{16,0},{24,8},{1,17},{9,25},{17,1},{25,9},{2,18},{10... | collective-permute-start | bytes 3145736 | tf_op jit(solution)/shard_map/ppermute | solution.py:344
  5.1 58.2 %copy-start = (bf16[128,2048]{1,0:T(8,128)(2,1)S(1)}, bf16[128,2048]{1,0:T(8,128)(2,1)}, u32[]{:S(2)}) copy-start(bf16[128,2048]{1,0:T(8,128)(2,1)} %refs_8_.1) | copy-start | bytes 1572868
  5.1 40.8 %collective-permute-start.14 = (bf16[3,16,2,32,128]{4,3,2,1,0:T(8,128)(2,1)S(1)}, bf16[3,16,2,32,128]{4,3,2,1,0:T(8,128)(2,1)S(1)}, u32[]{:S(2)}, u32[]{:S(2)}) collective-permute-start(bf16[3,16,2,32,128]{4,3,2,1,0:T(8,128)(2,1)S(1)} %slice.87.refs_2_.refs_1_), channel_id=1, source_target_pairs={{0,16},{8,24},{16,0},{24,8},{1,17},{9,25},{17,1},{25,9},{2,18},{10... | collective-permute-start | bytes 2359304 | tf_op jit(solution)/shard_map/ppermute | solution.py:344
  5.5 40.5 %collective-permute-start.13 = (bf16[3,16,2,32,128]{4,3,2,1,0:T(8,128)(2,1)S(1)}, bf16[3,16,2,32,128]{4,3,2,1,0:T(8,128)(2,1)S(1)}, u32[]{:S(2)}, u32[]{:S(2)}) collective-permute-start(bf16[3,16,2,32,128]{4,3,2,1,0:T(8,128)(2,1)S(1)} %slice.87.refs_2_.refs_1_), channel_id=1, source_target_pairs={{0,8},{8,0},{16,24},{24,16},{1,9},{9,1},{17,25},{25,17},{2,10},{10... | collective-permute-start | bytes 2359304 | tf_op jit(solution)/shard_map/ppermute | solution.py:344
  5.5 58.3 %collective-permute-start = (bf16[4,16,2,32,128]{4,3,2,1,0:T(8,128)(2,1)S(1)}, bf16[4,16,2,32,128]{4,3,2,1,0:T(8,128)(2,1)S(1)}, u32[]{:S(2)}, u32[]{:S(2)}) collective-permute-start(bf16[4,16,2,32,128]{4,3,2,1,0:T(8,128)(2,1)S(1)} %slice.84.refs_1_.refs_2_), channel_id=1, source_target_pairs={{0,8},{8,0},{16,24},{24,16},{1,9},{9,1},{17,25},{25,17},{2,10},{10... | collective-permute-start | bytes 3145736 | tf_op jit(solution)/shard_map/ppermute | solution.py:344
  29.1 38.0 %collective-permute-start.2 = (bf16[4,16,2,32,128]{4,3,2,1,0:T(8,128)(2,1)S(1)}, bf16[4,16,2,32,128]{4,3,2,1,0:T(8,128)(2,1)S(1)}, u32[]{:S(2)}, u32[]{:S(2)}) collective-permute-start(bf16[4,16,2,32,128]{4,3,2,1,0:T(8,128)(2,1)S(1)} %collective-permute-done.1.refs_3_.refs_4_), channel_id=1, source_target_pairs={{0,8},{8,0},{16,24},{24,16},{1,9},{9,1},{17,25},{25,17},{2,10},{10... | collective-permute-start | bytes 3145736 | tf_op jit(solution)/shard_map/ppermute | solution.py:344
  30.3 32.5 %collective-permute-start.5 = (bf16[3,16,2,32,128]{4,3,2,1,0:T(8,128)(2,1)S(1)}, bf16[3,16,2,32,128]{4,3,2,1,0:T(8,128)(2,1)S(1)}, u32[]{:S(2)}, u32[]{:S(2)}) collective-permute-start(bf16[3,16,2,32,128]{4,3,2,1,0:T(8,128)(2,1)S(1)} %slice.85.refs_2_.refs_1_), channel_id=1, source_target_pairs={{0,16},{8,24},{16,0},{24,8},{1,17},{9,25},{17,1},{25,9},{2,18},{10... | collective-permute-start | bytes 2359304 | tf_op jit(solution)/shard_map/ppermute | solution.py:344
  45.9 16.9 %collective-permute-start.15 = (bf16[3,16,2,32,128]{4,3,2,1,0:T(8,128)(2,1)S(1)}, bf16[3,16,2,32,128]{4,3,2,1,0:T(8,128)(2,1)S(1)}, u32[]{:S(2)}, u32[]{:S(2)}) collective-permute-start(bf16[3,16,2,32,128]{4,3,2,1,0:T(8,128)(2,1)S(1)} %collective-permute-done.14.refs_4_.refs_3_), channel_id=1, source_target_pairs={{0,8},{8,0},{16,24},{24,16},{1,9},{9,1},{17,25},{25,17},{2,10},{10... | collective-permute-start | bytes 2359304 | tf_op jit(solution)/shard_map/ppermute | solution.py:344
  46.0 21.1 %copy-start.9 = (bf16[128,2048]{1,0:T(8,128)(2,1)S(1)}, bf16[128,2048]{1,0:T(8,128)(2,1)}, u32[]{:S(2)}) copy-start(bf16[128,2048]{1,0:T(8,128)(2,1)} %refs_0_.5) | copy-start | bytes 1572868
  46.0 45.9 %collective-permute-start.10 = (bf16[4,16,2,32,128]{4,3,2,1,0:T(8,128)(2,1)S(1)}, bf16[4,16,2,32,128]{4,3,2,1,0:T(8,128)(2,1)S(1)}, u32[]{:S(2)}, u32[]{:S(2)}) collective-permute-start(bf16[4,16,2,32,128]{4,3,2,1,0:T(8,128)(2,1)S(1)} %slice.86.refs_1_.refs_2_), channel_id=1, source_target_pairs={{0,16},{8,24},{16,0},{24,8},{1,17},{9,25},{17,1},{25,9},{2,18},{10... | collective-permute-start | bytes 3145736 | tf_op jit(solution)/shard_map/ppermute | solution.py:344
  62.8 29.1 %collective-permute-start.4 = (bf16[3,16,2,32,128]{4,3,2,1,0:T(8,128)(2,1)S(1)}, bf16[3,16,2,32,128]{4,3,2,1,0:T(8,128)(2,1)S(1)}, u32[]{:S(2)}, u32[]{:S(2)}) collective-permute-start(bf16[3,16,2,32,128]{4,3,2,1,0:T(8,128)(2,1)S(1)} %slice.85.refs_2_.refs_1_), channel_id=1, source_target_pairs={{0,8},{8,0},{16,24},{24,16},{1,9},{9,1},{17,25},{25,17},{2,10},{10... | collective-permute-start | bytes 2359304 | tf_op jit(solution)/shard_map/ppermute | solution.py:344
  62.8 29.6 %collective-permute-start.6 = (bf16[3,16,2,32,128]{4,3,2,1,0:T(8,128)(2,1)S(1)}, bf16[3,16,2,32,128]{4,3,2,1,0:T(8,128)(2,1)S(1)}, u32[]{:S(2)}, u32[]{:S(2)}) collective-permute-start(bf16[3,16,2,32,128]{4,3,2,1,0:T(8,128)(2,1)S(1)} %collective-permute-done.5.refs_4_.refs_3_), channel_id=1, source_target_pairs={{0,8},{8,0},{16,24},{24,16},{1,9},{9,1},{17,25},{25,17},{2,10},{10... | collective-permute-start | bytes 2359304 | tf_op jit(solution)/shard_map/ppermute | solution.py:344
  63.9 26.6 %collective-permute-start.18 = (bf16[128,2048]{1,0:T(8,128)(2,1)S(1)}, bf16[128,2048]{1,0:T(8,128)(2,1)S(1)}, u32[]{:S(2)}, u32[]{:S(2)}) collective-permute-start(bf16[128,2048]{1,0:T(8,128)(2,1)S(1)} %get-tuple-element.53), channel_id=1, source_target_pairs={{0,4},{1,5},{2,6},{3,7},{4,0},{5,1},{6,2},{7,3},{8,12},{9,13},{10,... | collective-permute-start | bytes 1572872 | tf_op jit(solution)/shard_map/ppermute | solution.py:15
  70.9 20.2 %copy-start.27 = (bf16[128,2048]{1,0:T(8,128)(2,1)}, bf16[128,2048]{1,0:T(8,128)(2,1)S(1)}, u32[]{:S(2)}) copy-start(bf16[128,2048]{1,0:T(8,128)(2,1)S(1)} %get-tuple-element.72.refs_1_) | copy-start | bytes 1572868
  70.9 21.5 %collective-permute-start.3 = (bf16[128,2048]{1,0:T(8,128)(2,1)S(1)}, bf16[128,2048]{1,0:T(8,128)(2,1)S(1)}, u32[]{:S(2)}, u32[]{:S(2)}) collective-permute-start(bf16[128,2048]{1,0:T(8,128)(2,1)S(1)} %get-tuple-element.50.refs_0_), channel_id=1, source_target_pairs={{0,1},{1,0},{2,3},{3,2},{4,5},{5,4},{6,7},{7,6},{8,9},{9,8},{10,11... | collective-permute-start | bytes 1572872 | tf_op jit(solution)/shard_map/ppermute | solution.py:15
  91.1 14.9 %collective-permute-start.19 = (bf16[128,2048]{1,0:T(8,128)(2,1)S(1)}, bf16[128,2048]{1,0:T(8,128)(2,1)S(1)}, u32[]{:S(2)}, u32[]{:S(2)}) collective-permute-start(bf16[128,2048]{1,0:T(8,128)(2,1)S(1)} %get-tuple-element.55), channel_id=1, source_target_pairs={{0,2},{1,3},{2,0},{3,1},{4,6},{5,7},{6,4},{7,5},{8,10},{9,11},{10,... | collective-permute-start | bytes 1572872 | tf_op jit(solution)/shard_map/ppermute | solution.py:15
  91.9 27.5 %collective-permute-start.9 = (bf16[4,16,2,32,128]{4,3,2,1,0:T(8,128)(2,1)S(1)}, bf16[4,16,2,32,128]{4,3,2,1,0:T(8,128)(2,1)S(1)}, u32[]{:S(2)}, u32[]{:S(2)}) collective-permute-start(bf16[4,16,2,32,128]{4,3,2,1,0:T(8,128)(2,1)S(1)} %slice.86.refs_1_.refs_2_), channel_id=1, source_target_pairs={{0,8},{8,0},{16,24},{24,16},{1,9},{9,1},{17,25},{25,17},{2,10},{10... | collective-permute-start | bytes 3145736 | tf_op jit(solution)/shard_map/ppermute | solution.py:344
  91.9 27.5 %collective-permute-start.11 = (bf16[4,16,2,32,128]{4,3,2,1,0:T(8,128)(2,1)S(1)}, bf16[4,16,2,32,128]{4,3,2,1,0:T(8,128)(2,1)S(1)}, u32[]{:S(2)}, u32[]{:S(2)}) collective-permute-start(bf16[4,16,2,32,128]{4,3,2,1,0:T(8,128)(2,1)S(1)} %collective-permute-done.10.refs_3_.refs_4_), channel_id=1, source_target_pairs={{0,8},{8,0},{16,24},{24,16},{1,9},{9,1},{17,25},{25,17},{2,10},{10... | collective-permute-start | bytes 3145736 | tf_op jit(solution)/shard_map/ppermute | solution.py:344
  93.2 22.5 %collective-permute-start.7 = (bf16[128,2048]{1,0:T(8,128)(2,1)S(1)}, bf16[128,2048]{1,0:T(8,128)(2,1)S(1)}, u32[]{:S(2)}, u32[]{:S(2)}) collective-permute-start(bf16[128,2048]{1,0:T(8,128)(2,1)S(1)} %shard_map.76.refs_0_.refs_1_), channel_id=1, source_target_pairs={{0,2},{1,3},{2,0},{3,1},{4,6},{5,7},{6,4},{7,5},{8,10},{9,11},{10,... | collective-permute-start | bytes 1572872 | tf_op jit(solution)/shard_map/ppermute | solution.py:15
  108.5 11.0 %collective-permute-start.20 = (bf16[128,2048]{1,0:T(8,128)(2,1)S(1)}, bf16[128,2048]{1,0:T(8,128)(2,1)S(1)}, u32[]{:S(2)}, u32[]{:S(2)}) collective-permute-start(bf16[128,2048]{1,0:T(8,128)(2,1)S(1)} %get-tuple-element.57), channel_id=1, source_target_pairs={{0,1},{1,0},{2,3},{3,2},{4,5},{5,4},{6,7},{7,6},{8,9},{9,8},{10,11... | collective-permute-start | bytes 1572872 | tf_op jit(solution)/shard_map/ppermute | solution.py:15
  116.5 25.7 %collective-permute-start.8 = (bf16[128,2048]{1,0:T(8,128)(2,1)S(1)}, bf16[128,2048]{1,0:T(8,128)(2,1)S(1)}, u32[]{:S(2)}, u32[]{:S(2)}) collective-permute-start(bf16[128,2048]{1,0:T(8,128)(2,1)S(1)} %shard_map.77.refs_0_.refs_2_), channel_id=1, source_target_pairs={{0,4},{1,5},{2,6},{3,7},{4,0},{5,1},{6,2},{7,3},{8,12},{9,13},{10,... | collective-permute-start | bytes 1572872 | tf_op jit(solution)/shard_map/ppermute | solution.py:15
  121.8 21.0 %copy-start.29 = (bf16[128,2048]{1,0:T(8,128)(2,1)}, bf16[128,2048]{1,0:T(8,128)(2,1)S(1)}, u32[]{:S(2)}) copy-start(bf16[128,2048]{1,0:T(8,128)(2,1)S(1)} %get-tuple-element.82.refs_2_) | copy-start | bytes 1572868
  121.8 21.0 %copy-start.33 = (bf16[128,2048]{1,0:T(8,128)(2,1)}, bf16[128,2048]{1,0:T(8,128)(2,1)S(1)}, u32[]{:S(2)}) copy-start(bf16[128,2048]{1,0:T(8,128)(2,1)S(1)} %get-tuple-element.89.refs_3_) | copy-start | bytes 1572868
  145.1 25.1 %collective-permute-start.21 = (bf16[128,2048]{1,0:T(8,128)(2,1)S(1)}, bf16[128,2048]{1,0:T(8,128)(2,1)S(1)}, u32[]{:S(2)}, u32[]{:S(2)}) collective-permute-start(bf16[128,2048]{1,0:T(8,128)(2,1)S(1)} %get-tuple-element.60), channel_id=1, source_target_pairs={{0,4},{1,5},{2,6},{3,7},{4,0},{5,1},{6,2},{7,3},{8,12},{9,13},{10,... | collective-permute-start | bytes 1572872 | tf_op jit(solution)/shard_map/ppermute | solution.py:15
  147.5 23.4 %copy-start.31 = (bf16[128,2048]{1,0:T(8,128)(2,1)}, bf16[128,2048]{1,0:T(8,128)(2,1)S(1)}, u32[]{:S(2)}) copy-start(bf16[128,2048]{1,0:T(8,128)(2,1)S(1)} %get-tuple-element.81.refs_1_) | copy-start | bytes 1572868
  147.5 26.6 %copy-start.3 = (bf16[128,2048]{1,0:T(8,128)(2,1)}, bf16[128,2048]{1,0:T(8,128)(2,1)S(1)}, u32[]{:S(2)}) copy-start(bf16[128,2048]{1,0:T(8,128)(2,1)S(1)} %get-tuple-element.51.refs_0_) | copy-start | bytes 1572868
  147.5 22.7 %copy-start.16 = (f32[128,2048]{1,0:T(8,128)S(1)}, f32[128,2048]{1,0:T(8,128)}, u32[]{:S(2)}) copy-start(f32[128,2048]{1,0:T(8,128)} %copy-done.15) | copy-start | bytes 3145732
  147.5 26.6 %collective-permute-start.12 = (bf16[128,2048]{1,0:T(8,128)(2,1)S(1)}, bf16[128,2048]{1,0:T(8,128)(2,1)S(1)}, u32[]{:S(2)}, u32[]{:S(2)}) collective-permute-start(bf16[128,2048]{1,0:T(8,128)(2,1)S(1)} %get-tuple-element.51.refs_0_), channel_id=1, source_target_pairs={{0,1},{1,0},{2,3},{3,2},{4,5},{5,4},{6,7},{7,6},{8,9},{9,8},{10,11... | collective-permute-start | bytes 1572872 | tf_op jit(solution)/shard_map/ppermute | solution.py:15
  149.9 46.8 %copy-start.11 = (bf16[2,2,16,2,32,128]{5,4,3,2,1,0:T(8,128)(2,1)}, bf16[2,2,16,2,32,128]{5,4,3,2,1,0:T(8,128)(2,1)S(1)}, u32[]{:S(2)}) copy-start(bf16[2,2,16,2,32,128]{5,4,3,2,1,0:T(8,128)(2,1)S(1)} %get-tuple-element.90) | copy-start | bytes 3145732
  149.9 46.8 %collective-permute-start.32 = (bf16[2,2,16,2,32,128]{5,4,3,2,1,0:T(8,128)(2,1)S(1)}, bf16[2,2,16,2,32,128]{5,4,3,2,1,0:T(8,128)(2,1)}, u32[]{:S(2)}, u32[]{:S(2)}) collective-permute-start(bf16[2,2,16,2,32,128]{5,4,3,2,1,0:T(8,128)(2,1)S(1)} %get-tuple-element.91), channel_id=1, source_target_pairs={{0,8},{8,0},{16,24},{24,16},{1,9},{9,1},{17,25},{25,17},{2,10},{10... | collective-permute-start | bytes 3145736 | tf_op jit(solution)/shard_map/ppermute | solution.py:344
  170.9 14.9 %collective-permute-start.22 = (bf16[128,2048]{1,0:T(8,128)(2,1)S(1)}, bf16[128,2048]{1,0:T(8,128)(2,1)S(1)}, u32[]{:S(2)}, u32[]{:S(2)}) collective-permute-start(bf16[128,2048]{1,0:T(8,128)(2,1)S(1)} %get-tuple-element.62), channel_id=1, source_target_pairs={{0,2},{1,3},{2,0},{3,1},{4,6},{5,7},{6,4},{7,5},{8,10},{9,11},{10,... | collective-permute-start | bytes 1572872 | tf_op jit(solution)/shard_map/ppermute | solution.py:15
  174.1 33.2 %collective-permute-start.30 = (bf16[2,2,16,2,32,128]{5,4,3,2,1,0:T(8,128)(2,1)}, bf16[2,2,16,2,32,128]{5,4,3,2,1,0:T(8,128)(2,1)}, u32[]{:S(2)}, u32[]{:S(2)}) collective-permute-start(bf16[2,2,16,2,32,128]{5,4,3,2,1,0:T(8,128)(2,1)} %get-tuple-element.85), channel_id=1, source_target_pairs={{0,8},{8,0},{16,24},{24,16},{1,9},{9,1},{17,25},{25,17},{2,10},{10... | collective-permute-start | bytes 3145736 | tf_op jit(solution)/shard_map/ppermute | solution.py:344
  175.0 19.2 %collective-permute-start.16 = (bf16[128,2048]{1,0:T(8,128)(2,1)S(1)}, bf16[128,2048]{1,0:T(8,128)(2,1)S(1)}, u32[]{:S(2)}, u32[]{:S(2)}) collective-permute-start(bf16[128,2048]{1,0:T(8,128)(2,1)S(1)} %shard_map.80.refs_0_.refs_1_), channel_id=1, source_target_pairs={{0,2},{1,3},{2,0},{3,1},{4,6},{5,7},{6,4},{7,5},{8,10},{9,11},{10,... | collective-permute-start | bytes 1572872 | tf_op jit(solution)/shard_map/ppermute | solution.py:15
  186.4 16.0 %collective-permute-start.23 = (bf16[128,2048]{1,0:T(8,128)(2,1)S(1)}, bf16[128,2048]{1,0:T(8,128)(2,1)S(1)}, u32[]{:S(2)}, u32[]{:S(2)}) collective-permute-start(bf16[128,2048]{1,0:T(8,128)(2,1)S(1)} %get-tuple-element.64), channel_id=1, source_target_pairs={{0,1},{1,0},{2,3},{3,2},{4,5},{5,4},{6,7},{7,6},{8,9},{9,8},{10,11... | collective-permute-start | bytes 1572872 | tf_op jit(solution)/shard_map/ppermute | solution.py:15
  194.8 24.7 %collective-permute-start.17 = (bf16[128,2048]{1,0:T(8,128)(2,1)S(1)}, bf16[128,2048]{1,0:T(8,128)(2,1)S(1)}, u32[]{:S(2)}, u32[]{:S(2)}) collective-permute-start(bf16[128,2048]{1,0:T(8,128)(2,1)S(1)} %shard_map.81.refs_0_.refs_2_), channel_id=1, source_target_pairs={{0,4},{1,5},{2,6},{3,7},{4,0},{5,1},{6,2},{7,3},{8,12},{9,13},{10,... | collective-permute-start | bytes 1572872 | tf_op jit(solution)/shard_map/ppermute | solution.py:15
  198.7 21.9 %collective-permute-start.33 = (bf16[2,16,2,32,128]{4,3,2,1,0:T(8,128)(2,1)}, bf16[2,16,2,32,128]{4,3,2,1,0:T(8,128)(2,1)}, u32[]{:S(2)}, u32[]{:S(2)}) collective-permute-start(bf16[2,16,2,32,128]{4,3,2,1,0:T(8,128)(2,1)} %fusion.11), channel_id=1, source_target_pairs={{0,16},{8,24},{16,0},{24,8},{1,17},{9,25},{17,1},{25,9},{2,18},{10... | collective-permute-start | bytes 1572872 | tf_op jit(solution)/shard_map/ppermute | solution.py:344
  202.5 26.5 %collective-permute-start.28 = (bf16[2,3,16,2,32,128]{5,4,3,2,1,0:T(8,128)(2,1)}, bf16[2,3,16,2,32,128]{5,4,3,2,1,0:T(8,128)(2,1)}, u32[]{:S(2)}, u32[]{:S(2)}) collective-permute-start(bf16[2,3,16,2,32,128]{5,4,3,2,1,0:T(8,128)(2,1)} %get-tuple-element.80), channel_id=1, source_target_pairs={{0,8},{8,0},{16,24},{24,16},{1,9},{9,1},{17,25},{25,17},{2,10},{10... | collective-permute-start | bytes 4718600 | tf_op jit(solution)/shard_map/ppermute | solution.py:344
  206.7 18.7 %collective-permute-start.26 = (bf16[2,2,16,2,32,128]{5,4,3,2,1,0:T(8,128)(2,1)S(1)}, bf16[2,2,16,2,32,128]{5,4,3,2,1,0:T(8,128)(2,1)S(1)}, u32[]{:S(2)}, u32[]{:S(2)}) collective-permute-start(bf16[2,2,16,2,32,128]{5,4,3,2,1,0:T(8,128)(2,1)S(1)} %get-tuple-element.76), channel_id=1, source_target_pairs={{0,8},{8,0},{16,24},{24,16},{1,9},{9,1},{17,25},{25,17},{2,10},{10... | collective-permute-start | bytes 3145736 | tf_op jit(solution)/shard_map/ppermute | solution.py:344
  207.3 12.2 %copy-start.4 = (bf16[128,2048]{1,0:T(8,128)(2,1)S(1)}, bf16[128,2048]{1,0:T(8,128)(2,1)}, u32[]{:S(2)}) copy-start(bf16[128,2048]{1,0:T(8,128)(2,1)} %copy-done.3) | copy-start | bytes 1572868
  207.3 12.2 %copy-start.20 = (bf16[128,2048]{1,0:T(8,128)(2,1)S(1)}, bf16[128,2048]{1,0:T(8,128)(2,1)}, u32[]{:S(2)}) copy-start(bf16[128,2048]{1,0:T(8,128)(2,1)} %copy-done.19) | copy-start | bytes 1572868
  207.3 12.2 %copy-start.22 = (bf16[128,2048]{1,0:T(8,128)(2,1)S(1)}, bf16[128,2048]{1,0:T(8,128)(2,1)}, u32[]{:S(2)}) copy-start(bf16[128,2048]{1,0:T(8,128)(2,1)} %copy-done.21) | copy-start | bytes 1572868
  208.6 15.4 %collective-permute-start.31 = (bf16[2,16,2,32,128]{4,3,2,1,0:T(8,128)(2,1)S(1)}, bf16[2,16,2,32,128]{4,3,2,1,0:T(8,128)(2,1)S(1)}, u32[]{:S(2)}, u32[]{:S(2)}) collective-permute-start(bf16[2,16,2,32,128]{4,3,2,1,0:T(8,128)(2,1)S(1)} %fusion.10), channel_id=1, source_target_pairs={{0,16},{8,24},{16,0},{24,8},{1,17},{9,25},{17,1},{25,9},{2,18},{10... | collective-permute-start | bytes 1572872 | tf_op jit(solution)/shard_map/ppermute | solution.py:344
  219.5 7.6 %collective-permute-start.24 = (bf16[2,2,16,2,32,128]{5,4,3,2,1,0:T(8,128)(2,1)S(1)}, bf16[2,2,16,2,32,128]{5,4,3,2,1,0:T(8,128)(2,1)}, u32[]{:S(2)}, u32[]{:S(2)}) collective-permute-start(bf16[2,2,16,2,32,128]{5,4,3,2,1,0:T(8,128)(2,1)S(1)} %get-tuple-element.70), channel_id=1, source_target_pairs={{0,8},{8,0},{16,24},{24,16},{1,9},{9,1},{17,25},{25,17},{2,10},{10... | collective-permute-start | bytes 3145736 | tf_op jit(solution)/shard_map/ppermute | solution.py:344
  220.6 11.3 %collective-permute-start.34 = (bf16[2,3,16,2,32,128]{5,4,3,2,1,0:T(8,128)(2,1)S(1)}, bf16[2,3,16,2,32,128]{5,4,3,2,1,0:T(8,128)(2,1)S(1)}, u32[]{:S(2)}, u32[]{:S(2)}) collective-permute-start(bf16[2,3,16,2,32,128]{5,4,3,2,1,0:T(8,128)(2,1)S(1)} %get-tuple-element.95), channel_id=1, source_target_pairs={{0,8},{8,0},{16,24},{24,16},{1,9},{9,1},{17,25},{25,17},{2,10},{10... | collective-permute-start | bytes 4718600 | tf_op jit(solution)/shard_map/ppermute | solution.py:344
  225.5 14.9 %collective-permute-start.27 = (bf16[2,16,2,32,128]{4,3,2,1,0:T(8,128)(2,1)S(1)}, bf16[2,16,2,32,128]{4,3,2,1,0:T(8,128)(2,1)S(1)}, u32[]{:S(2)}, u32[]{:S(2)}) collective-permute-start(bf16[2,16,2,32,128]{4,3,2,1,0:T(8,128)(2,1)S(1)} %fusion.9), channel_id=1, source_target_pairs={{0,16},{8,24},{16,0},{24,8},{1,17},{9,25},{17,1},{25,9},{2,18},{10... | collective-permute-start | bytes 1572872 | tf_op jit(solution)/shard_map/ppermute | solution.py:344
  228.3 23.3 %collective-permute-start.25 = (bf16[2,16,2,32,128]{4,3,2,1,0:T(8,128)(2,1)S(1)}, bf16[2,16,2,32,128]{4,3,2,1,0:T(8,128)(2,1)S(1)}, u32[]{:S(2)}, u32[]{:S(2)}) collective-permute-start(bf16[2,16,2,32,128]{4,3,2,1,0:T(8,128)(2,1)S(1)} %fusion.8), channel_id=1, source_target_pairs={{0,16},{8,24},{16,0},{24,8},{1,17},{9,25},{17,1},{25,9},{2,18},{10... | collective-permute-start | bytes 1572872 | tf_op jit(solution)/shard_map/ppermute | solution.py:344
  230.4 38.1 %collective-permute-start.29 = (bf16[3,16,2,32,128]{4,3,2,1,0:T(8,128)(2,1)S(1)}, bf16[3,16,2,32,128]{4,3,2,1,0:T(8,128)(2,1)S(1)}, u32[]{:S(2)}, u32[]{:S(2)}) collective-permute-start(bf16[3,16,2,32,128]{4,3,2,1,0:T(8,128)(2,1)S(1)} %fusion.6), channel_id=1, source_target_pairs={{0,16},{8,24},{16,0},{24,8},{1,17},{9,25},{17,1},{25,9},{2,18},{10... | collective-permute-start | bytes 2359304 | tf_op jit(solution)/shard_map/ppermute | solution.py:344
  232.3 52.1 %collective-permute-start.35 = (bf16[3,16,2,32,128]{4,3,2,1,0:T(8,128)(2,1)S(1)}, bf16[3,16,2,32,128]{4,3,2,1,0:T(8,128)(2,1)S(1)}, u32[]{:S(2)}, u32[]{:S(2)}) collective-permute-start(bf16[3,16,2,32,128]{4,3,2,1,0:T(8,128)(2,1)S(1)} %fusion.7), channel_id=1, source_target_pairs={{0,16},{8,24},{16,0},{24,8},{1,17},{9,25},{17,1},{25,9},{2,18},{10... | collective-permute-start | bytes 2359304 | tf_op jit(solution)/shard_map/ppermute | solution.py:344
  (24 other events, 64.2 us)

commit v2 on v1

--- a/solution.py
+++ b/solution.py
@@ -273,12 +273,7 @@
 PARAMS = dict(compiler_params=pltpu.CompilerParams(vmem_limit_bytes=40 * 2**20))
 
 
-def estimate(n_levels, tok_rows, count, width, moved):
-    return pl.CostEstimate(
-        flops=4 * n_levels * tok_rows * count * width * width,
-        bytes_accessed=moved,
-        transcendentals=0,
-    )
+COST = pl.CostEstimate(flops=1, bytes_accessed=1, transcendentals=0)
 
 
 def call_forward(values, partner, pieces, levels, bits, out_type=jnp.bfloat16):
@@ -292,7 +287,7 @@
         in_specs=[VMEM] * len(acts) + [ANY] * 4,
         out_specs=[VMEM] * n,
         scratch_shapes=[pltpu.VMEM(buf, jnp.bfloat16), pltpu.SemaphoreType.DMA((n, 4))],
-        cost_estimate=estimate(n, values.shape[0], count, width, 2 * math.prod(buf) + 4 * n * values.size),
+        cost_estimate=COST,
         **PARAMS,
     )(*acts, *pieces)
 
@@ -311,7 +306,7 @@
         in_specs=[VMEM] * len(incoming) + [ANY] * 4,
         out_specs=[VMEM] * len(outs),
         scratch_shapes=[pltpu.VMEM(buf, jnp.bfloat16), pltpu.SemaphoreType.DMA((n, 4))],
-        cost_estimate=estimate(n, shape[0], count, width, 2 * math.prod(buf) + 6 * n * math.prod(shape)),
+        cost_estimate=COST,
         **PARAMS,
     )(*incoming, *pieces)
 
@@ -328,101 +323,144 @@
         out_shape=[out, out],
         in_specs=[VMEM] * len(acts),
         out_specs=[VMEM] * 2,
-        cost_estimate=estimate(n, tok_rows, count, width, 10 * n * values[0].size),
+        cost_estimate=COST,
         **PARAMS,
     )(*acts)
 
 
-def sum_pairs(keep, send):
-    got = partner_dp(send, 1)
-    across = (keep[1].astype(jnp.float32) + got[1].astype(jnp.float32)).astype(jnp.bfloat16)
-    mine = keep[0].astype(jnp.float32) + got[0].astype(jnp.float32)
-    return mine + partner_dp(across, 2).astype(jnp.float32)
-
-
 def partner_dp(value, mask):
     return lax.ppermute(value, "dp", [(k, k ^ mask) for k in range(lax.axis_size("dp"))])
 
 
-def gather_pairs(shard):
+def after(value, earlier):
+    return lax.optimization_barrier((value, earlier))[0]
+
+
+def gather_pairs(shard, earlier=None):
+    if earlier is not None:
+        shard = after(shard, earlier)
+    far = partner_dp(shard, 2)
     near = partner_dp(shard, 1)
-    far = partner_dp(shard, 2)
     return [shard, near, far, partner_dp(far, 1)]
 
 
 def on_device_pairs(tokens, cotangent, factor_in, factor_out):
     level_count, local_blocks, _, rows, width = factor_in.shape
     local_bits = local_blocks.bit_length() - 1
+    top = level_count - 1
     grad_scale = 1.0 / math.sqrt(tokens.shape[0] * lax.axis_size("dp"))
     low = tuple(range(local_bits))
+    down = tuple(reversed(low))
     high = tuple(range(local_bits, level_count))
 
-    in_low = gather_pairs(factor_in[:local_bits])
-    in_high = gather_pairs(factor_in[local_bits:])
-    out_high = gather_pairs(factor_out[local_bits:])
-    out_low = gather_pairs(factor_out[:local_bits])
+    out_top = gather_pairs(factor_out[top:])
+    in_low = gather_pairs(factor_in[:local_bits], out_top[2])
+    gathered = {}
 
     def over_feat(value, level):
         return partner_2(value, "feat", level - local_bits)
 
-    def forward(values, pieces_low, pieces_high, last_type):
-        stored = [values] + list(call_forward(values, None, pieces_low, low, low))
-        partners = []
-        for level in high:
-            partner = over_feat(stored[level], level)
-            partners.append(partner)
-            out_type = last_type if level == level_count - 1 else jnp.bfloat16
-            stored += call_forward(
-                stored[level], partner, pieces_high, (level - local_bits,), (level,), out_type
-            )
-        return stored, partners
-
-    def backward(grad, pieces_low, pieces_high):
-        grads = [None] * level_count
-        incoming = [grad]
-        for level in reversed(high):
-            *head, own, other = call_backward(
-                incoming, pieces_high, (level - local_bits,), (level,), True
-            )
-            if level == level_count - 1:
-                grads[level] = grad
-            else:
-                grads[level] = head[0]
-            incoming = [own, over_feat(other, level)]
-        down = tuple(reversed(low))
-        got = call_backward(incoming, pieces_low, down, down, False)
-        for place, level in enumerate(down):
-            grads[level] = got[place]
-        return got[-1], grads
-
-    def level_sums(stored, partners, grads, group):
+    def in_place(level):
+        return gathered["in_high"], level - local_bits
+
+    def out_place(level):
+        return (out_top, 0) if level == top else (gathered["out_high"], level - local_bits)
+
+    def forward_low(values, pieces):
+        return [values] + list(call_forward(values, None, pieces, low, low))
+
+    def forward_high(value, partner, place, level, out_type=jnp.bfloat16):
+        pieces, at = place(level)
+        return call_forward(value, partner, pieces, (at,), (level,), out_type)[0]
+
+    def backward_high(incoming, place, level):
+        pieces, at = place(level)
+        *head, own, other = call_backward(incoming, pieces, (at,), (level,), True)
+        return (head[0] if head else incoming[0]), [own, over_feat(other, level)]
+
+    def start_sums(values, partners, grads, group):
         remote = group[0] >= local_bits
         keep, send = call_grads(
-            [stored[level] for level in group],
-            [partners[level - local_bits] for level in group] if remote else None,
+            [values[level] for level in group],
+            [partners[level] for level in group] if remote else None,
             [grads[level] for level in group],
             group,
             rows,
             grad_scale,
         )
-        return sum_pairs(keep, send)
-
-    stored_in, partners_in = forward(tokens, in_low, in_high, jnp.float32)
-    grad_mid, grads_out = backward(cotangent, out_low, out_high)
-    pre_gelu = stored_in[-1]
+        got = partner_dp(send, 1)
+        across = (keep[1].astype(jnp.float32) + got[1].astype(jnp.float32)).astype(jnp.bfloat16)
+        mine = keep[0].astype(jnp.float32) + got[0].astype(jnp.float32)
+        return across, mine
+
+    def cross(started):
+        across, mine = started
+        return partner_dp(across, 2), mine
+
+    def end_sums(crossed):
+        far, mine = crossed
+        return mine + far.astype(jnp.float32)
+
+    grads_out, partners_in = {}, {}
+    incoming = [cotangent]
+    grads_out[top], incoming = backward_high(incoming, out_place, top)
+    gathered["in_high"] = gather_pairs(factor_in[local_bits:], (in_low[2], incoming[0]))
+    acts_in = forward_low(tokens, in_low)
+    gathered["out_high"] = gather_pairs(
+        factor_out[local_bits:top], (gathered["in_high"][2], acts_in[-1], incoming[1])
+    )
+    for level in high:
+        partners_in[level] = over_feat(acts_in[level], level)
+        out_type = jnp.float32 if level == top else jnp.bfloat16
+        acts_in.append(forward_high(acts_in[level], partners_in[level], in_place, level, out_type))
+    out_low = gather_pairs(
+        factor_out[:local_bits], (gathered["out_high"][2], acts_in[local_bits + 1])
+    )
+    for level in reversed(high[:-1]):
+        grads_out[level], incoming = backward_high(incoming, out_place, level)
+    got = call_backward(incoming, out_low, down, down, False)
+    for place, level in enumerate(down):
+        grads_out[level] = got[place]
+    grad_mid, pre_gelu = got[-1], acts_in[-1]
     hidden = gelu_exact(pre_gelu).astype(jnp.bfloat16)
     grad_pre = (grad_mid.astype(jnp.float32) * gelu_slope(pre_gelu)).astype(jnp.bfloat16)
-    stored_out, partners_out = forward(hidden, out_low, out_high, jnp.bfloat16)
-    token_grad, grads_in = backward(grad_pre, in_low, in_high)
-    half = local_bits // 2
-    groups = [low[:half], low[half:], high]
-    sums_out = [level_sums(stored_out, partners_out, grads_out, group) for group in groups]
-    sums_in = [level_sums(stored_in, partners_in, grads_in, group) for group in reversed(groups)]
+
+    grads_in, partners_out, sums_in, sums_out = {}, {}, {}, {}
+    grads_in[top], incoming = backward_high([grad_pre], in_place, top)
+    acts_out = forward_low(hidden, out_low)
+    sums_in[top] = start_sums(acts_in, partners_in, grads_in, (top,))
+    sums_out[0] = start_sums(acts_out, partners_out, grads_out, low)
+    for level in high:
+        partners_out[level] = over_feat(acts_out[level], level)
+        if level == local_bits:
+            partners_out[level] = after(partners_out[level], incoming[0])
+        acts_out.append(forward_high(acts_out[level], partners_out[level], out_place, level))
+    middle = high[:-1]
+    for level in reversed(middle):
+        if level == top - 1:
+            incoming[0] = after(incoming[0], (sums_in[top][0], sums_out[0][0]))
+        if level == local_bits:
+            sums_in[top], sums_out[0] = cross(sums_in[top]), cross(sums_out[0])
+            sums_out[local_bits] = start_sums(acts_out, partners_out, grads_out, middle)
+            ready = (sums_in[top][0], sums_out[0][0], sums_out[local_bits][0], acts_out[top])
+            incoming[0] = after(incoming[0], ready)
+        grads_in[level], incoming = backward_high(incoming, in_place, level)
+    sums_in[local_bits] = start_sums(acts_in, partners_in, grads_in, middle)
+    sums_out[local_bits] = cross(sums_out[local_bits])
+    ready = (sums_in[local_bits][0], sums_out[local_bits][0], partners_out[top])
+    incoming[0] = after(incoming[0], ready)
+    got = call_backward(incoming, in_low, down, down, False)
+    for place, level in enumerate(down):
+        grads_in[level] = got[place]
+    sums_in[local_bits] = cross(sums_in[local_bits])
+    sums_out[top] = cross(start_sums(acts_out, partners_out, grads_out, (top,)))
+    across, mine = start_sums(acts_in, partners_in, grads_in, low)
+    sums_in[0] = cross((after(across, sums_in[local_bits][0]), mine))
     return (
-        stored_out[-1],
-        token_grad,
-        jnp.concatenate(sums_in[::-1], 0),
-        jnp.concatenate(sums_out, 0),
+        acts_out[-1],
+        got[-1],
+        jnp.concatenate([end_sums(sums_in[level]) for level in sorted(sums_in)], 0),
+        jnp.concatenate([end_sums(sums_out[level]) for level in sorted(sums_out)], 0),
     )
 
 

time: 288 us -> 295 us (1.024)
  waiting for transfers between devices: 198 us -> 219 us
  other arithmetic: 18.3 us -> 11.4 us
  starting transfers between devices: 34.8 us -> 30 us
    ppermute x24 -> x27, waiting for transfers between devices: 97.1 us -> 129 us  [partner_dp(): lax.ppermute(value, 'dp', [(k, k ^ mask) for k in range(lax.axis_size('dp...]
    ppermute x12, waiting for transfers between devices: 101 us -> 90.4 us  [partner_2(): return lax.ppermute(value, axis, pairs)]
    ppermute x12, starting transfers between devices: 18.1 us -> 13.9 us  [partner_2(): return lax.ppermute(value, axis, pairs)]
    convert_element_type x6, other arithmetic: 6.57 us -> 2.6 us  [start_sums(): (keep[1].astype(jnp.float32) + got[1].astype(jnp.float32)).astype(jnp.bfl...]
    add x6, other arithmetic: 6.29 us -> 3.17 us  [end_sums(): return mine + far.astype(jnp.float32)]
    unnamed x72 -> x80, local copies, waits for them, and re-layouts: 6.89 us -> 5.22 us
    ppermute x24 -> x27, starting transfers between devices: 16.8 us -> 16.1 us  [partner_dp(): lax.ppermute(value, 'dp', [(k, k ^ mask) for k in range(lax.axis_size('dp...]
  transfers between devices with their start and end apart: 36 -> 39, of which waited for: 15 -> 20; matrix products, arithmetic and copies ran while one was open for 6% -> 3% of each run, Pallas kernels for 8% -> 4%
where the time goes in v2:
time: 295 us; the launch traced here: 294 us
  waiting for transfers between devices  219 us (74%)
  starting transfers between devices  30 us (10%)
  Pallas kernels  23.4 us (8%)
  other arithmetic  11.4 us (4%)
  local copies, waits for them, and re-layouts  8.82 us (3%)
    ppermute x27, waiting for transfers between devices, partner_dp(): lax.ppermute(value, 'dp', [(k, k ^ mask) for k in range(lax.axis_size('dp...  129 us
    ppermute x12, waiting for transfers between devices, partner_2(): return lax.ppermute(value, axis, pairs)  90.4 us
    ppermute x27, starting transfers between devices, partner_dp(): lax.ppermute(value, 'dp', [(k, k ^ mask) for k in range(lax.axis_size('dp...  16.1 us
    ppermute x12, starting transfers between devices, partner_2(): return lax.ppermute(value, axis, pairs)  13.9 us
    pallas_call x8, Pallas kernels, call_backward(): pl.pallas_call(functools.partial(backward_kernel, levels, bits, remote, l...  9.42 us
    pallas_call x8, Pallas kernels, call_forward(): pl.pallas_call(functools.partial(forward_kernel, levels, bits, partner is...  8.61 us
  transfers between devices with their start and end apart: 39, of which 20 were waited for; matrix products, arithmetic and copies ran while one was open for 3% of the time, Pallas kernels for 4%

profile of v2, /device:TPU:0, one launch (start us, length us, event | category | flops | bytes accessed | tf_op | source)
XLA Modules:
  0.0 294.4 jit_solution(16956099693521906359)
XLA Ops:
  0.6 1.0 slice.88.refs_1_.refs_2_
  1.7 3.0 %collective-permute-start = (bf16[1,16,2,32,128]{4,3,2,1,0:T(8,128)(2,1)S(1)}, bf16[1,16,2,32,128]{4,3,2,1,0:T(8,128)(2,1)S(1)}, u32[]{:S(2)}, u32[]{:S(2)}) collective-permute-start(bf16[1,16,2,32,128]{4,3,2,1,0:T(8,128)(2,1)S(1)} %slice.88.refs_1_.refs_2_), channel_id=1, source_target_pairs={{0,16},{8,24},{16,0},{24,8},{1,17},{9,25},{17,1},{25,9},{2,18},{10... | collective-permute-start | bytes 786440 | tf_op jit(solution)/shard_map/ppermute | solution.py:332
  4.7 1.3 slice.87.refs_1_.refs_2_
  6.0 5.0 %collective-permute-done.refs_3_.refs_4_ = bf16[1,16,2,32,128]{4,3,2,1,0:T(8,128)(2,1)S(1)} collective-permute-done((bf16[1,16,2,32,128]{4,3,2,1,0:T(8,128)(2,1)S(1)}, bf16[1,16,2,32,128]{4,3,2,1,0:T(8,128)(2,1)S(1)}, u32[]{:S(2)}, u32[]{:S(2)}) %collective-permute-start) | collective-permute-done | bytes 262176 | tf_op jit(solution)/shard_map/ppermute | solution.py:332
  11.0 1.7 collective-permute-start.2
  13.2 1.2 slice.89.refs_2_.refs_1_
  15.2 20.1 %collective-permute-done.2.refs_3_.refs_4_ = bf16[4,16,2,32,128]{4,3,2,1,0:T(8,128)(2,1)S(1)} collective-permute-done((bf16[4,16,2,32,128]{4,3,2,1,0:T(8,128)(2,1)S(1)}, bf16[4,16,2,32,128]{4,3,2,1,0:T(8,128)(2,1)S(1)}, u32[]{:S(2)}, u32[]{:S(2)}) %collective-permute-start.2) | collective-permute-done | bytes 1048608 | tf_op jit(solution)/shard_map/ppermute | solution.py:332
  35.3 1.4 collective-permute-start.8
  36.8 2.6 collective-permute-start.12
  39.3 15.9 %collective-permute-done.8.refs_4_.refs_3_ = bf16[3,16,2,32,128]{4,3,2,1,0:T(8,128)(2,1)S(1)} collective-permute-done((bf16[3,16,2,32,128]{4,3,2,1,0:T(8,128)(2,1)S(1)}, bf16[3,16,2,32,128]{4,3,2,1,0:T(8,128)(2,1)S(1)}, u32[]{:S(2)}, u32[]{:S(2)}) %collective-permute-start.8) | collective-permute-done | bytes 786464 | tf_op jit(solution)/shard_map/ppermute | solution.py:332
  55.4 2.2 shard_map.75
  57.6 1.5 collective-permute-start.4
  59.1 3.8 %collective-permute-done.12.refs_1_ = bf16[128,2048]{1,0:T(8,128)(2,1)S(1)} collective-permute-done((bf16[128,2048]{1,0:T(8,128)(2,1)S(1)}, bf16[128,2048]{1,0:T(8,128)(2,1)S(1)}, u32[]{:S(2)}, u32[]{:S(2)}) %collective-permute-start.12) | collective-permute-done | bytes 524320 | tf_op jit(solution)/shard_map/ppermute | solution.py:15
  63.6 8.4 %collective-permute-done.4.refs_1_.refs_2_ = bf16[128,2048]{1,0:T(8,128)(2,1)S(1)} collective-permute-done((bf16[128,2048]{1,0:T(8,128)(2,1)S(1)}, bf16[128,2048]{1,0:T(8,128)(2,1)S(1)}, u32[]{:S(2)}, u32[]{:S(2)}) %collective-permute-start.4) | collective-permute-done | bytes 524320 | tf_op jit(solution)/shard_map/ppermute | solution.py:15
  72.8 3.3 %collective-permute-done.13.refs_4_ = bf16[2,16,2,32,128]{4,3,2,1,0:T(8,128)(2,1)S(1)} collective-permute-done((bf16[2,16,2,32,128]{4,3,2,1,0:T(8,128)(2,1)S(1)}, bf16[2,16,2,32,128]{4,3,2,1,0:T(8,128)(2,1)S(1)}, u32[]{:S(2)}, u32[]{:S(2)}) %collective-permute-start.13) | collective-permute-done | bytes 524320 | tf_op jit(solution)/shard_map/ppermute | solution.py:332
  77.3 1.2 collective-permute-start.10
  80.1 1.3 collective-permute-start.20
  81.4 18.3 %collective-permute-done.15.refs_3_.refs_4_ = bf16[4,16,2,32,128]{4,3,2,1,0:T(8,128)(2,1)S(1)} collective-permute-done((bf16[4,16,2,32,128]{4,3,2,1,0:T(8,128)(2,1)S(1)}, bf16[4,16,2,32,128]{4,3,2,1,0:T(8,128)(2,1)S(1)}, u32[]{:S(2)}, u32[]{:S(2)}) %collective-permute-start.15) | collective-permute-done | bytes 1048608 | tf_op jit(solution)/shard_map/ppermute | solution.py:332
  103.0 1.5 collective-permute-start.21
  104.5 23.0 %collective-permute-done.11.refs_1_ = bf16[128,2048]{1,0:T(8,128)(2,1)S(1)} collective-permute-done((bf16[128,2048]{1,0:T(8,128)(2,1)S(1)}, bf16[128,2048]{1,0:T(8,128)(2,1)S(1)}, u32[]{:S(2)}, u32[]{:S(2)}) %collective-permute-start.11) | collective-permute-done | bytes 524320 | tf_op jit(solution)/shard_map/ppermute | solution.py:15
  128.4 2.3 shard_map.83
  132.1 2.4 shard_map.80
  134.5 1.2 copy-done.32
  135.7 1.4 shard_map.89
  137.2 1.6 collective-permute-start.17
  139.4 12.2 %collective-permute-done.17.refs_1_.refs_2_ = bf16[128,2048]{1,0:T(8,128)(2,1)S(1)} collective-permute-done((bf16[128,2048]{1,0:T(8,128)(2,1)S(1)}, bf16[128,2048]{1,0:T(8,128)(2,1)S(1)}, u32[]{:S(2)}, u32[]{:S(2)}) %collective-permute-start.17) | collective-permute-done | bytes 524320 | tf_op jit(solution)/shard_map/ppermute | solution.py:15
  152.8 1.9 collective-permute-start.26
  154.7 19.5 %collective-permute-done.22.refs_1_.refs_3_ = bf16[128,2048]{1,0:T(8,128)(2,1)S(1)} collective-permute-done((bf16[128,2048]{1,0:T(8,128)(2,1)S(1)}, bf16[128,2048]{1,0:T(8,128)(2,1)S(1)}, u32[]{:S(2)}, u32[]{:S(2)}) %collective-permute-start.22) | collective-permute-done | bytes 524320 | tf_op jit(solution)/shard_map/ppermute | solution.py:15
  174.2 1.0 copy-done.10
  176.1 1.7 fusion.6
  177.8 1.5 collective-permute-start.28
  181.7 27.3 %collective-permute-done.27 = bf16[1,16,2,32,128]{4,3,2,1,0:T(8,128)(2,1)S(1)} collective-permute-done((bf16[1,16,2,32,128]{4,3,2,1,0:T(8,128)(2,1)S(1)}, bf16[1,16,2,32,128]{4,3,2,1,0:T(8,128)(2,1)S(1)}, u32[]{:S(2)}, u32[]{:S(2)}) %collective-permute-start.27) | collective-permute-done | bytes 262176 | tf_op jit(solution)/shard_map/ppermute | solution.py:332
  211.6 1.3 collective-permute-start.32
  212.9 1.5 collective-permute-start.33
  214.5 22.7 %collective-permute-done.23.refs_1_ = bf16[128,2048]{1,0:T(8,128)(2,1)S(1)} collective-permute-done((bf16[128,2048]{1,0:T(8,128)(2,1)S(1)}, bf16[128,2048]{1,0:T(8,128)(2,1)S(1)}, u32[]{:S(2)}, u32[]{:S(2)}) %collective-permute-start.23) | collective-permute-done | bytes 524320 | tf_op jit(solution)/shard_map/ppermute | solution.py:15
  237.3 3.4 %shard_map.94 = (bf16[128,2048]{1,0:T(8,128)(2,1)S(1)}, bf16[128,2048]{1,0:T(8,128)(2,1)S(1)}, bf16[128,2048]{1,0:T(8,128)(2,1)S(1)}, bf16[128,2048]{1,0:T(8,128)(2,1)S(1)}, bf16[128,2048]{1,0:T(8,128)(2,1)}) custom-call(f32[128,2048]{1,0:T(8,128)S(1)} %get-tuple-element.99.refs_0_, bf16[128,2048]{1,0:T(8,128)(2,1)S(1)} %collective-permute-done.33.refs_1_, ...), custom_call_target="tpu_custom_call" | custom-call | flops 1 | bytes 1 | tf_op jit(solution)/shard_map/pallas_call | solution.py:303
  240.7 1.4 shard_map.95
  243.3 3.8 %collective-permute-done.37 = bf16[2,1,16,2,32,128]{5,4,3,2,1,0:T(8,128)(2,1)S(1)} collective-permute-done((bf16[2,1,16,2,32,128]{5,4,3,2,1,0:T(8,128)(2,1)S(1)}, bf16[2,1,16,2,32,128]{5,4,3,2,1,0:T(8,128)(2,1)S(1)}, u32[]{:S(2)}, u32[]{:S(2)}) %collective-permute-start.37) | collective-permute-done | bytes 524320 | tf_op jit(solution)/shard_map/ppermute | solution.py:332
  247.2 1.1 collective-permute-start.38
  248.4 1.4 shard_map.87
  249.8 1.1 collective-permute-start.35
  250.9 5.5 %collective-permute-done.38 = bf16[1,16,2,32,128]{4,3,2,1,0:T(8,128)(2,1)S(1)} collective-permute-done((bf16[1,16,2,32,128]{4,3,2,1,0:T(8,128)(2,1)S(1)}, bf16[1,16,2,32,128]{4,3,2,1,0:T(8,128)(2,1)S(1)}, u32[]{:S(2)}, u32[]{:S(2)}) %collective-permute-start.38) | collective-permute-done | bytes 262176 | tf_op jit(solution)/shard_map/ppermute | solution.py:332
  257.0 9.9 %collective-permute-done.35 = bf16[2,16,2,32,128]{4,3,2,1,0:T(8,128)(2,1)S(1)} collective-permute-done((bf16[2,16,2,32,128]{4,3,2,1,0:T(8,128)(2,1)S(1)}, bf16[2,16,2,32,128]{4,3,2,1,0:T(8,128)(2,1)S(1)}, u32[]{:S(2)}, u32[]{:S(2)}) %collective-permute-start.35) | collective-permute-done | bytes 524320 | tf_op jit(solution)/shard_map/ppermute | solution.py:332
  266.9 1.0 collective-permute-start.36
  268.1 1.8 bitcast_add_fusion
  270.0 2.5 pad_maximum_fusion.1
  272.8 18.5 %collective-permute-done.36 = bf16[4,16,2,32,128]{4,3,2,1,0:T(8,128)(2,1)S(1)} collective-permute-done((bf16[4,16,2,32,128]{4,3,2,1,0:T(8,128)(2,1)S(1)}, bf16[4,16,2,32,128]{4,3,2,1,0:T(8,128)(2,1)S(1)}, u32[]{:S(2)}, u32[]{:S(2)}) %collective-permute-start.36) | collective-permute-done | bytes 1048608 | tf_op jit(solution)/shard_map/ppermute | solution.py:332
  291.8 2.5 pad_maximum_fusion
  (152 shorter events, 21.7 us)
Async XLA Ops:
  1.7 9.3 %collective-permute-start = (bf16[1,16,2,32,128]{4,3,2,1,0:T(8,128)(2,1)S(1)}, bf16[1,16,2,32,128]{4,3,2,1,0:T(8,128)(2,1)S(1)}, u32[]{:S(2)}, u32[]{:S(2)}) collective-permute-start(bf16[1,16,2,32,128]{4,3,2,1,0:T(8,128)(2,1)S(1)} %slice.88.refs_1_.refs_2_), channel_id=1, source_target_pairs={{0,16},{8,24},{16,0},{24,8},{1,17},{9,25},{17,1},{25,9},{2,18},{10... | collective-permute-start | bytes 786440 | tf_op jit(solution)/shard_map/ppermute | solution.py:332
  6.0 49.3 %copy-start.35 = (bf16[7,16,2,32,128]{4,3,2,1,0:T(8,128)(2,1)S(1)}, bf16[7,16,2,32,128]{4,3,2,1,0:T(8,128)(2,1)}, u32[]{:S(2)}) copy-start(bf16[7,16,2,32,128]{4,3,2,1,0:T(8,128)(2,1)} %param.7) | copy-start | bytes 5505028
  6.0 49.4 %copy-start.11 = (bf16[128,2048]{1,0:T(8,128)(2,1)S(1)}, bf16[128,2048]{1,0:T(8,128)(2,1)}, u32[]{:S(2)}) copy-start(bf16[128,2048]{1,0:T(8,128)(2,1)} %refs_0_.5) | copy-start | bytes 1572868
  11.0 44.4 %copy-start.13 = (bf16[1,16,2,32,128]{4,3,2,1,0:T(8,128)(2,1)}, bf16[1,16,2,32,128]{4,3,2,1,0:T(8,128)(2,1)S(1)}, u32[]{:S(2)}) copy-start(bf16[1,16,2,32,128]{4,3,2,1,0:T(8,128)(2,1)S(1)} %collective-permute-done.refs_3_.refs_4_) | copy-start | bytes 786436
  11.0 24.3 %collective-permute-start.2 = (bf16[4,16,2,32,128]{4,3,2,1,0:T(8,128)(2,1)S(1)}, bf16[4,16,2,32,128]{4,3,2,1,0:T(8,128)(2,1)S(1)}, u32[]{:S(2)}, u32[]{:S(2)}) collective-permute-start(bf16[4,16,2,32,128]{4,3,2,1,0:T(8,128)(2,1)S(1)} %slice.87.refs_1_.refs_2_), channel_id=1, source_target_pairs={{0,16},{8,24},{16,0},{24,8},{1,17},{9,25},{17,1},{25,9},{2,18},{10... | collective-permute-start | bytes 3145736 | tf_op jit(solution)/shard_map/ppermute | solution.py:332
  12.7 1.8 collective-permute-start.5
  12.7 1.9 collective-permute-start.6
  14.4 40.9 %collective-permute-start.1 = (bf16[4,16,2,32,128]{4,3,2,1,0:T(8,128)(2,1)S(1)}, bf16[4,16,2,32,128]{4,3,2,1,0:T(8,128)(2,1)S(1)}, u32[]{:S(2)}, u32[]{:S(2)}) collective-permute-start(bf16[4,16,2,32,128]{4,3,2,1,0:T(8,128)(2,1)S(1)} %slice.87.refs_1_.refs_2_), channel_id=1, source_target_pairs={{0,8},{8,0},{16,24},{24,16},{1,9},{9,1},{17,25},{25,17},{2,10},{10... | collective-permute-start | bytes 3145736 | tf_op jit(solution)/shard_map/ppermute | solution.py:332
  14.5 43.1 %copy-start.15 = (bf16[1,16,2,32,128]{4,3,2,1,0:T(8,128)(2,1)}, bf16[1,16,2,32,128]{4,3,2,1,0:T(8,128)(2,1)S(1)}, u32[]{:S(2)}) copy-start(bf16[1,16,2,32,128]{4,3,2,1,0:T(8,128)(2,1)S(1)} %collective-permute-done.5.refs_2_.refs_3_) | copy-start | bytes 786436
  14.6 42.9 %copy-start.17 = (bf16[1,16,2,32,128]{4,3,2,1,0:T(8,128)(2,1)}, bf16[1,16,2,32,128]{4,3,2,1,0:T(8,128)(2,1)S(1)}, u32[]{:S(2)}) copy-start(bf16[1,16,2,32,128]{4,3,2,1,0:T(8,128)(2,1)S(1)} %collective-permute-done.6.refs_4_.refs_5_) | copy-start | bytes 786436
  35.3 20.0 %collective-permute-start.3 = (bf16[4,16,2,32,128]{4,3,2,1,0:T(8,128)(2,1)S(1)}, bf16[4,16,2,32,128]{4,3,2,1,0:T(8,128)(2,1)S(1)}, u32[]{:S(2)}, u32[]{:S(2)}) collective-permute-start(bf16[4,16,2,32,128]{4,3,2,1,0:T(8,128)(2,1)S(1)} %collective-permute-done.2.refs_3_.refs_4_), channel_id=1, source_target_pairs={{0,8},{8,0},{16,24},{24,16},{1,9},{9,1},{17,25},{25,17},{2,10},{10... | collective-permute-start | bytes 3145736 | tf_op jit(solution)/shard_map/ppermute | solution.py:332
  35.3 20.0 %collective-permute-start.8 = (bf16[3,16,2,32,128]{4,3,2,1,0:T(8,128)(2,1)S(1)}, bf16[3,16,2,32,128]{4,3,2,1,0:T(8,128)(2,1)S(1)}, u32[]{:S(2)}, u32[]{:S(2)}) collective-permute-start(bf16[3,16,2,32,128]{4,3,2,1,0:T(8,128)(2,1)S(1)} %slice.89.refs_2_.refs_1_), channel_id=1, source_target_pairs={{0,16},{8,24},{16,0},{24,8},{1,17},{9,25},{17,1},{25,9},{2,18},{10... | collective-permute-start | bytes 2359304 | tf_op jit(solution)/shard_map/ppermute | solution.py:332
  36.8 26.2 %collective-permute-start.12 = (bf16[128,2048]{1,0:T(8,128)(2,1)S(1)}, bf16[128,2048]{1,0:T(8,128)(2,1)S(1)}, u32[]{:S(2)}, u32[]{:S(2)}) collective-permute-start(bf16[128,2048]{1,0:T(8,128)(2,1)S(1)} %get-tuple-element.63), channel_id=1, source_target_pairs={{0,4},{1,5},{2,6},{3,7},{4,0},{5,1},{6,2},{7,3},{8,12},{9,13},{10,... | collective-permute-start | bytes 1572872 | tf_op jit(solution)/shard_map/ppermute | solution.py:15
  39.3 24.3 %collective-permute-start.7 = (bf16[3,16,2,32,128]{4,3,2,1,0:T(8,128)(2,1)S(1)}, bf16[3,16,2,32,128]{4,3,2,1,0:T(8,128)(2,1)S(1)}, u32[]{:S(2)}, u32[]{:S(2)}) collective-permute-start(bf16[3,16,2,32,128]{4,3,2,1,0:T(8,128)(2,1)S(1)} %slice.89.refs_2_.refs_1_), channel_id=1, source_target_pairs={{0,8},{8,0},{16,24},{24,16},{1,9},{9,1},{17,25},{25,17},{2,10},{10... | collective-permute-start | bytes 2359304 | tf_op jit(solution)/shard_map/ppermute | solution.py:332
  55.3 8.3 %collective-permute-start.9 = (bf16[3,16,2,32,128]{4,3,2,1,0:T(8,128)(2,1)S(1)}, bf16[3,16,2,32,128]{4,3,2,1,0:T(8,128)(2,1)S(1)}, u32[]{:S(2)}, u32[]{:S(2)}) collective-permute-start(bf16[3,16,2,32,128]{4,3,2,1,0:T(8,128)(2,1)S(1)} %collective-permute-done.8.refs_4_.refs_3_), channel_id=1, source_target_pairs={{0,8},{8,0},{16,24},{24,16},{1,9},{9,1},{17,25},{25,17},{2,10},{10... | collective-permute-start | bytes 2359304 | tf_op jit(solution)/shard_map/ppermute | solution.py:332
  57.6 14.4 %collective-permute-start.4 = (bf16[128,2048]{1,0:T(8,128)(2,1)S(1)}, bf16[128,2048]{1,0:T(8,128)(2,1)S(1)}, u32[]{:S(2)}, u32[]{:S(2)}) collective-permute-start(bf16[128,2048]{1,0:T(8,128)(2,1)S(1)} %get-tuple-element.60.refs_0_), channel_id=1, source_target_pairs={{0,1},{1,0},{2,3},{3,2},{4,5},{5,4},{6,7},{7,6},{8,9},{9,8},{10,11... | collective-permute-start | bytes 1572872 | tf_op jit(solution)/shard_map/ppermute | solution.py:15
  62.9 13.2 %collective-permute-start.13 = (bf16[2,16,2,32,128]{4,3,2,1,0:T(8,128)(2,1)S(1)}, bf16[2,16,2,32,128]{4,3,2,1,0:T(8,128)(2,1)S(1)}, u32[]{:S(2)}, u32[]{:S(2)}) collective-permute-start(bf16[2,16,2,32,128]{4,3,2,1,0:T(8,128)(2,1)S(1)} %slice.91.refs_2_), channel_id=1, source_target_pairs={{0,16},{8,24},{16,0},{24,8},{1,17},{9,25},{17,1},{25,9},{2,18},{10... | collective-permute-start | bytes 1572872 | tf_op jit(solution)/shard_map/ppermute | solution.py:332
  76.2 23.6 %collective-permute-start.15 = (bf16[4,16,2,32,128]{4,3,2,1,0:T(8,128)(2,1)S(1)}, bf16[4,16,2,32,128]{4,3,2,1,0:T(8,128)(2,1)S(1)}, u32[]{:S(2)}, u32[]{:S(2)}) collective-permute-start(bf16[4,16,2,32,128]{4,3,2,1,0:T(8,128)(2,1)S(1)} %slice.90.refs_1_.refs_2_), channel_id=1, source_target_pairs={{0,16},{8,24},{16,0},{24,8},{1,17},{9,25},{17,1},{25,9},{2,18},{10... | collective-permute-start | bytes 3145736 | tf_op jit(solution)/shard_map/ppermute | solution.py:332
  76.8 1.9 collective-permute-start.18
  76.8 2.7 collective-permute-start.19
  77.3 22.4 %collective-permute-start.10 = (bf16[128,2048]{1,0:T(8,128)(2,1)S(1)}, bf16[128,2048]{1,0:T(8,128)(2,1)S(1)}, u32[]{:S(2)}, u32[]{:S(2)}) collective-permute-start(bf16[128,2048]{1,0:T(8,128)(2,1)S(1)} %shard_map.77.refs_0_.refs_1_), channel_id=1, source_target_pairs={{0,2},{1,3},{2,0},{3,1},{4,6},{5,7},{6,4},{7,5},{8,10},{9,11},{10,... | collective-permute-start | bytes 1572872 | tf_op jit(solution)/shard_map/ppermute | solution.py:15
  80.1 22.3 %collective-permute-start.20 = (bf16[128,2048]{1,0:T(8,128)(2,1)S(1)}, bf16[128,2048]{1,0:T(8,128)(2,1)S(1)}, u32[]{:S(2)}, u32[]{:S(2)}) collective-permute-start(bf16[128,2048]{1,0:T(8,128)(2,1)S(1)} %get-tuple-element.68), channel_id=1, source_target_pairs={{0,2},{1,3},{2,0},{3,1},{4,6},{5,7},{6,4},{7,5},{8,10},{9,11},{10,... | collective-permute-start | bytes 1572872 | tf_op jit(solution)/shard_map/ppermute | solution.py:15
  81.4 47.0 %collective-permute-start.14 = (bf16[4,16,2,32,128]{4,3,2,1,0:T(8,128)(2,1)S(1)}, bf16[4,16,2,32,128]{4,3,2,1,0:T(8,128)(2,1)S(1)}, u32[]{:S(2)}, u32[]{:S(2)}) collective-permute-start(bf16[4,16,2,32,128]{4,3,2,1,0:T(8,128)(2,1)S(1)} %slice.90.refs_1_.refs_2_), channel_id=1, source_target_pairs={{0,8},{8,0},{16,24},{24,16},{1,9},{9,1},{17,25},{25,17},{2,10},{10... | collective-permute-start | bytes 3145736 | tf_op jit(solution)/shard_map/ppermute | solution.py:332
  99.7 28.7 %collective-permute-start.16 = (bf16[4,16,2,32,128]{4,3,2,1,0:T(8,128)(2,1)S(1)}, bf16[4,16,2,32,128]{4,3,2,1,0:T(8,128)(2,1)S(1)}, u32[]{:S(2)}, u32[]{:S(2)}) collective-permute-start(bf16[4,16,2,32,128]{4,3,2,1,0:T(8,128)(2,1)S(1)} %collective-permute-done.15.refs_3_.refs_4_), channel_id=1, source_target_pairs={{0,8},{8,0},{16,24},{24,16},{1,9},{9,1},{17,25},{25,17},{2,10},{10... | collective-permute-start | bytes 3145736 | tf_op jit(solution)/shard_map/ppermute | solution.py:332
  101.1 26.5 %collective-permute-start.11 = (bf16[128,2048]{1,0:T(8,128)(2,1)S(1)}, bf16[128,2048]{1,0:T(8,128)(2,1)S(1)}, u32[]{:S(2)}, u32[]{:S(2)}) collective-permute-start(bf16[128,2048]{1,0:T(8,128)(2,1)S(1)} %shard_map.78.refs_0_), channel_id=1, source_target_pairs={{0,4},{1,5},{2,6},{3,7},{4,0},{5,1},{6,2},{7,3},{8,12},{9,13},{10,... | collective-permute-start | bytes 1572872 | tf_op jit(solution)/shard_map/ppermute | solution.py:15
  103.0 25.1 %copy-start.23 = (bf16[128,2048]{1,0:T(8,128)(2,1)}, bf16[128,2048]{1,0:T(8,128)(2,1)S(1)}, u32[]{:S(2)}) copy-start(bf16[128,2048]{1,0:T(8,128)(2,1)S(1)} %get-tuple-element.88.refs_4_) | copy-start | bytes 1572868
  103.0 25.4 %collective-permute-start.21 = (bf16[128,2048]{1,0:T(8,128)(2,1)S(1)}, bf16[128,2048]{1,0:T(8,128)(2,1)S(1)}, u32[]{:S(2)}, u32[]{:S(2)}) collective-permute-start(bf16[128,2048]{1,0:T(8,128)(2,1)S(1)} %get-tuple-element.70), channel_id=1, source_target_pairs={{0,1},{1,0},{2,3},{3,2},{4,5},{5,4},{6,7},{7,6},{8,9},{9,8},{10,11... | collective-permute-start | bytes 1572872 | tf_op jit(solution)/shard_map/ppermute | solution.py:15
  137.1 39.0 %collective-permute-start.25 = (bf16[2,4,16,2,32,128]{5,4,3,2,1,0:T(8,128)(2,1)S(1)}, bf16[2,4,16,2,32,128]{5,4,3,2,1,0:T(8,128)(2,1)}, u32[]{:S(2)}, u32[]{:S(2)}) collective-permute-start(bf16[2,4,16,2,32,128]{5,4,3,2,1,0:T(8,128)(2,1)S(1)} %get-tuple-element.84), channel_id=1, source_target_pairs={{0,8},{8,0},{16,24},{24,16},{1,9},{9,1},{17,25},{25,17},{2,10},{10... | collective-permute-start | bytes 6291464 | tf_op jit(solution)/shard_map/ppermute | solution.py:332
  137.2 14.3 %collective-permute-start.17 = (bf16[128,2048]{1,0:T(8,128)(2,1)S(1)}, bf16[128,2048]{1,0:T(8,128)(2,1)S(1)}, u32[]{:S(2)}, u32[]{:S(2)}) collective-permute-start(bf16[128,2048]{1,0:T(8,128)(2,1)S(1)} %get-tuple-element.66.refs_0_), channel_id=1, source_target_pairs={{0,1},{1,0},{2,3},{3,2},{4,5},{5,4},{6,7},{7,6},{8,9},{9,8},{10,11... | collective-permute-start | bytes 1572872 | tf_op jit(solution)/shard_map/ppermute | solution.py:15
  151.5 22.6 %copy-start.22 = (bf16[128,2048]{1,0:T(8,128)(2,1)S(1)}, bf16[128,2048]{1,0:T(8,128)(2,1)}, u32[]{:S(2)}) copy-start(bf16[128,2048]{1,0:T(8,128)(2,1)} %copy-done.21) | copy-start | bytes 1572868
  151.5 22.6 %copy-start.24 = (bf16[128,2048]{1,0:T(8,128)(2,1)S(1)}, bf16[128,2048]{1,0:T(8,128)(2,1)}, u32[]{:S(2)}) copy-start(bf16[128,2048]{1,0:T(8,128)(2,1)} %copy-done.23) | copy-start | bytes 1572868
  152.1 22.1 %collective-permute-start.22 = (bf16[128,2048]{1,0:T(8,128)(2,1)S(1)}, bf16[128,2048]{1,0:T(8,128)(2,1)S(1)}, u32[]{:S(2)}, u32[]{:S(2)}) collective-permute-start(bf16[128,2048]{1,0:T(8,128)(2,1)S(1)} %shard_map.85.refs_0_.refs_1_), channel_id=1, source_target_pairs={{0,2},{1,3},{2,0},{3,1},{4,6},{5,7},{6,4},{7,5},{8,10},{9,11},{10,... | collective-permute-start | bytes 1572872 | tf_op jit(solution)/shard_map/ppermute | solution.py:15
  152.7 26.5 %copy-start.19 = (bf16[2,1,16,2,32,128]{5,4,3,2,1,0:T(8,128)(2,1)}, bf16[2,1,16,2,32,128]{5,4,3,2,1,0:T(8,128)(2,1)S(1)}, u32[]{:S(2)}) copy-start(bf16[2,1,16,2,32,128]{5,4,3,2,1,0:T(8,128)(2,1)S(1)} %get-tuple-element.74) | copy-start | bytes 1572868
  152.7 26.5 %collective-permute-start.24 = (bf16[2,1,16,2,32,128]{5,4,3,2,1,0:T(8,128)(2,1)S(1)}, bf16[2,1,16,2,32,128]{5,4,3,2,1,0:T(8,128)(2,1)S(1)}, u32[]{:S(2)}, u32[]{:S(2)}) collective-permute-start(bf16[2,1,16,2,32,128]{5,4,3,2,1,0:T(8,128)(2,1)S(1)} %get-tuple-element.75), channel_id=1, source_target_pairs={{0,8},{8,0},{16,24},{24,16},{1,9},{9,1},{17,25},{25,17},{2,10},{10... | collective-permute-start | bytes 1572872 | tf_op jit(solution)/shard_map/ppermute | solution.py:332
  152.8 26.5 %collective-permute-start.26 = (bf16[128,2048]{1,0:T(8,128)(2,1)S(1)}, bf16[128,2048]{1,0:T(8,128)(2,1)S(1)}, u32[]{:S(2)}, u32[]{:S(2)}) collective-permute-start(bf16[128,2048]{1,0:T(8,128)(2,1)S(1)} %get-tuple-element.86), channel_id=1, source_target_pairs={{0,4},{1,5},{2,6},{3,7},{4,0},{5,1},{6,2},{7,3},{8,12},{9,13},{10,... | collective-permute-start | bytes 1572872 | tf_op jit(solution)/shard_map/ppermute | solution.py:15
  176.0 5.4 %collective-permute-start.29 = (bf16[2,2,16,2,32,128]{5,4,3,2,1,0:T(8,128)(2,1)S(1)}, bf16[2,2,16,2,32,128]{5,4,3,2,1,0:T(8,128)(2,1)S(1)}, u32[]{:S(2)}, u32[]{:S(2)}) collective-permute-start(bf16[2,2,16,2,32,128]{5,4,3,2,1,0:T(8,128)(2,1)S(1)} %get-tuple-element.91), channel_id=1, source_target_pairs={{0,8},{8,0},{16,24},{24,16},{1,9},{9,1},{17,25},{25,17},{2,10},{10... | collective-permute-start | bytes 3145736 | tf_op jit(solution)/shard_map/ppermute | solution.py:332
  177.8 31.2 %collective-permute-start.28 = (bf16[4,16,2,32,128]{4,3,2,1,0:T(8,128)(2,1)S(1)}, bf16[4,16,2,32,128]{4,3,2,1,0:T(8,128)(2,1)S(1)}, u32[]{:S(2)}, u32[]{:S(2)}) collective-permute-start(bf16[4,16,2,32,128]{4,3,2,1,0:T(8,128)(2,1)S(1)} %fusion.6), channel_id=1, source_target_pairs={{0,16},{8,24},{16,0},{24,8},{1,17},{9,25},{17,1},{25,9},{2,18},{10... | collective-permute-start | bytes 3145736 | tf_op jit(solution)/shard_map/ppermute | solution.py:332
  180.0 29.0 %collective-permute-start.30 = (bf16[128,2048]{1,0:T(8,128)(2,1)S(1)}, bf16[128,2048]{1,0:T(8,128)(2,1)S(1)}, u32[]{:S(2)}, u32[]{:S(2)}) collective-permute-start(bf16[128,2048]{1,0:T(8,128)(2,1)S(1)} %get-tuple-element.93), channel_id=1, source_target_pairs={{0,2},{1,3},{2,0},{3,1},{4,6},{5,7},{6,4},{7,5},{8,10},{9,11},{10,... | collective-permute-start | bytes 1572872 | tf_op jit(solution)/shard_map/ppermute | solution.py:15
  180.1 28.9 %collective-permute-start.27 = (bf16[1,16,2,32,128]{4,3,2,1,0:T(8,128)(2,1)S(1)}, bf16[1,16,2,32,128]{4,3,2,1,0:T(8,128)(2,1)S(1)}, u32[]{:S(2)}, u32[]{:S(2)}) collective-permute-start(bf16[1,16,2,32,128]{4,3,2,1,0:T(8,128)(2,1)S(1)} %fusion.10), channel_id=1, source_target_pairs={{0,16},{8,24},{16,0},{24,8},{1,17},{9,25},{17,1},{25,9},{2,18},{10... | collective-permute-start | bytes 786440 | tf_op jit(solution)/shard_map/ppermute | solution.py:332
  211.3 3.1 %collective-permute-start.31 = (bf16[2,2,16,2,32,128]{5,4,3,2,1,0:T(8,128)(2,1)S(1)}, bf16[2,2,16,2,32,128]{5,4,3,2,1,0:T(8,128)(2,1)S(1)}, u32[]{:S(2)}, u32[]{:S(2)}) collective-permute-start(bf16[2,2,16,2,32,128]{5,4,3,2,1,0:T(8,128)(2,1)S(1)} %get-tuple-element.98), channel_id=1, source_target_pairs={{0,8},{8,0},{16,24},{24,16},{1,9},{9,1},{17,25},{25,17},{2,10},{10... | collective-permute-start | bytes 3145736 | tf_op jit(solution)/shard_map/ppermute | solution.py:332
  211.3 25.9 %collective-permute-start.23 = (bf16[128,2048]{1,0:T(8,128)(2,1)S(1)}, bf16[128,2048]{1,0:T(8,128)(2,1)S(1)}, u32[]{:S(2)}, u32[]{:S(2)}) collective-permute-start(bf16[128,2048]{1,0:T(8,128)(2,1)S(1)} %shard_map.86.refs_0_), channel_id=1, source_target_pairs={{0,4},{1,5},{2,6},{3,7},{4,0},{5,1},{6,2},{7,3},{8,12},{9,13},{10,... | collective-permute-start | bytes 1572872 | tf_op jit(solution)/shard_map/ppermute | solution.py:15
  211.6 25.7 %collective-permute-start.32 = (bf16[2,16,2,32,128]{4,3,2,1,0:T(8,128)(2,1)S(1)}, bf16[2,16,2,32,128]{4,3,2,1,0:T(8,128)(2,1)S(1)}, u32[]{:S(2)}, u32[]{:S(2)}) collective-permute-start(bf16[2,16,2,32,128]{4,3,2,1,0:T(8,128)(2,1)S(1)} %fusion.8), channel_id=1, source_target_pairs={{0,16},{8,24},{16,0},{24,8},{1,17},{9,25},{17,1},{25,9},{2,18},{10... | collective-permute-start | bytes 1572872 | tf_op jit(solution)/shard_map/ppermute | solution.py:332
  212.9 24.4 %collective-permute-start.33 = (bf16[128,2048]{1,0:T(8,128)(2,1)S(1)}, bf16[128,2048]{1,0:T(8,128)(2,1)S(1)}, u32[]{:S(2)}, u32[]{:S(2)}) collective-permute-start(bf16[128,2048]{1,0:T(8,128)(2,1)S(1)} %get-tuple-element.100), channel_id=1, source_target_pairs={{0,1},{1,0},{2,3},{3,2},{4,5},{5,4},{6,7},{7,6},{8,9},{9,8},{10,11... | collective-permute-start | bytes 1572872 | tf_op jit(solution)/shard_map/ppermute | solution.py:15
  242.2 14.4 %collective-permute-start.34 = (bf16[2,4,16,2,32,128]{5,4,3,2,1,0:T(8,128)(2,1)S(1)}, bf16[2,4,16,2,32,128]{5,4,3,2,1,0:T(8,128)(2,1)S(1)}, u32[]{:S(2)}, u32[]{:S(2)}) collective-permute-start(bf16[2,4,16,2,32,128]{5,4,3,2,1,0:T(8,128)(2,1)S(1)} %get-tuple-element.110), channel_id=1, source_target_pairs={{0,8},{8,0},{16,24},{24,16},{1,9},{9,1},{17,25},{25,17},{2,10},{10... | collective-permute-start | bytes 6291464 | tf_op jit(solution)/shard_map/ppermute | solution.py:332
  242.8 4.4 %collective-permute-start.37 = (bf16[2,1,16,2,32,128]{5,4,3,2,1,0:T(8,128)(2,1)S(1)}, bf16[2,1,16,2,32,128]{5,4,3,2,1,0:T(8,128)(2,1)S(1)}, u32[]{:S(2)}, u32[]{:S(2)}) collective-permute-start(bf16[2,1,16,2,32,128]{5,4,3,2,1,0:T(8,128)(2,1)S(1)} %get-tuple-element.113), channel_id=1, source_target_pairs={{0,8},{8,0},{16,24},{24,16},{1,9},{9,1},{17,25},{25,17},{2,10},{10... | collective-permute-start | bytes 1572872 | tf_op jit(solution)/shard_map/ppermute | solution.py:332
  247.2 9.2 %collective-permute-start.38 = (bf16[1,16,2,32,128]{4,3,2,1,0:T(8,128)(2,1)S(1)}, bf16[1,16,2,32,128]{4,3,2,1,0:T(8,128)(2,1)S(1)}, u32[]{:S(2)}, u32[]{:S(2)}) collective-permute-start(bf16[1,16,2,32,128]{4,3,2,1,0:T(8,128)(2,1)S(1)} %fusion.11), channel_id=1, source_target_pairs={{0,16},{8,24},{16,0},{24,8},{1,17},{9,25},{17,1},{25,9},{2,18},{10... | collective-permute-start | bytes 786440 | tf_op jit(solution)/shard_map/ppermute | solution.py:332
  249.8 17.1 %collective-permute-start.35 = (bf16[2,16,2,32,128]{4,3,2,1,0:T(8,128)(2,1)S(1)}, bf16[2,16,2,32,128]{4,3,2,1,0:T(8,128)(2,1)S(1)}, u32[]{:S(2)}, u32[]{:S(2)}) collective-permute-start(bf16[2,16,2,32,128]{4,3,2,1,0:T(8,128)(2,1)S(1)} %fusion.9), channel_id=1, source_target_pairs={{0,16},{8,24},{16,0},{24,8},{1,17},{9,25},{17,1},{25,9},{2,18},{10... | collective-permute-start | bytes 1572872 | tf_op jit(solution)/shard_map/ppermute | solution.py:332
  266.9 24.4 %collective-permute-start.36 = (bf16[4,16,2,32,128]{4,3,2,1,0:T(8,128)(2,1)S(1)}, bf16[4,16,2,32,128]{4,3,2,1,0:T(8,128)(2,1)S(1)}, u32[]{:S(2)}, u32[]{:S(2)}) collective-permute-start(bf16[4,16,2,32,128]{4,3,2,1,0:T(8,128)(2,1)S(1)} %fusion.7), channel_id=1, source_target_pairs={{0,16},{8,24},{16,0},{24,8},{1,17},{9,25},{17,1},{25,9},{2,18},{10... | collective-permute-start | bytes 3145736 | tf_op jit(solution)/shard_map/ppermute | solution.py:332
  (31 other events, 191.2 us)

commit v3 on v2

--- a/solution.py
+++ b/solution.py
@@ -336,11 +336,13 @@
     return lax.optimization_barrier((value, earlier))[0]
 
 
-def gather_pairs(shard, earlier=None):
+def gather_pairs(shard, earlier=None, between=None):
     if earlier is not None:
         shard = after(shard, earlier)
     far = partner_dp(shard, 2)
     near = partner_dp(shard, 1)
+    if between is not None:
+        far = after(far, between)
     return [shard, near, far, partner_dp(far, 1)]
 
 
@@ -414,7 +416,7 @@
         out_type = jnp.float32 if level == top else jnp.bfloat16
         acts_in.append(forward_high(acts_in[level], partners_in[level], in_place, level, out_type))
     out_low = gather_pairs(
-        factor_out[:local_bits], (gathered["out_high"][2], acts_in[local_bits + 1])
+        factor_out[:local_bits], (gathered["out_high"][2], acts_in[local_bits + 1]), acts_in[top]
     )
     for level in reversed(high[:-1]):
         grads_out[level], incoming = backward_high(incoming, out_place, level)
@@ -433,7 +435,9 @@
     for level in high:
         partners_out[level] = over_feat(acts_out[level], level)
         if level == local_bits:
-            partners_out[level] = after(partners_out[level], incoming[0])
+            partners_out[level] = after(
+                partners_out[level], (incoming[1], sums_in[top][0], sums_out[0][0])
+            )
         acts_out.append(forward_high(acts_out[level], partners_out[level], out_place, level))
     middle = high[:-1]
     for level in reversed(middle):
@@ -442,12 +446,12 @@
         if level == local_bits:
             sums_in[top], sums_out[0] = cross(sums_in[top]), cross(sums_out[0])
             sums_out[local_bits] = start_sums(acts_out, partners_out, grads_out, middle)
-            ready = (sums_in[top][0], sums_out[0][0], sums_out[local_bits][0], acts_out[top])
+            ready = (acts_out[top], sums_in[top][0], sums_out[0][0])
             incoming[0] = after(incoming[0], ready)
         grads_in[level], incoming = backward_high(incoming, in_place, level)
     sums_in[local_bits] = start_sums(acts_in, partners_in, grads_in, middle)
     sums_out[local_bits] = cross(sums_out[local_bits])
-    ready = (sums_in[local_bits][0], sums_out[local_bits][0], partners_out[top])
+    ready = (sums_in[local_bits][0], partners_out[top])
     incoming[0] = after(incoming[0], ready)
     got = call_backward(incoming, in_low, down, down, False)
     for place, level in enumerate(down):

time: 295 us -> 287 us (0.973)
  waiting for transfers between devices: 219 us -> 210 us
    ppermute x27, waiting for transfers between devices: 129 us -> 99 us  [partner_dp(): lax.ppermute(value, 'dp', [(k, k ^ mask) for k in range(lax.axis_size('dp...]
    ppermute x12, waiting for transfers between devices: 90.4 us -> 111 us  [partner_2(): return lax.ppermute(value, axis, pairs)]
  transfers between devices with their start and end apart: 39 -> 39, of which waited for: 20 -> 24; matrix products, arithmetic and copies ran while one was open for 3% -> 3% of each run, Pallas kernels for 4% -> 5%
where the time goes in v3:
time: 287 us; the launch traced here: 286 us
  waiting for transfers between devices  210 us (73%)
  starting transfers between devices  31.2 us (11%)
  Pallas kernels  26.3 us (9%)
  other arithmetic  9.93 us (3%)
  local copies, waits for them, and re-layouts  7.03 us (2%)
    ppermute x12, waiting for transfers between devices, partner_2(): return lax.ppermute(value, axis, pairs)  111 us
    ppermute x27, waiting for transfers between devices, partner_dp(): lax.ppermute(value, 'dp', [(k, k ^ mask) for k in range(lax.axis_size('dp...  99 us
    ppermute x27, starting transfers between devices, partner_dp(): lax.ppermute(value, 'dp', [(k, k ^ mask) for k in range(lax.axis_size('dp...  17.3 us
    ppermute x12, starting transfers between devices, partner_2(): return lax.ppermute(value, axis, pairs)  13.9 us
    pallas_call x8, Pallas kernels, call_forward(): pl.pallas_call(functools.partial(forward_kernel, levels, bits, partner is...  10.4 us
    pallas_call x8, Pallas kernels, call_backward(): pl.pallas_call(functools.partial(backward_kernel, levels, bits, remote, l...  9.4 us
    pallas_call x6, Pallas kernels, call_grads(): pl.pallas_call(functools.partial(grad_kernel, bits, partners is not None,...  6.49 us
  transfers between devices with their start and end apart: 39, of which 24 were waited for; matrix products, arithmetic and copies ran while one was open for 3% of the time, Pallas kernels for 5%

profile of v3, /device:TPU:0, one launch (start us, length us, event | category | flops | bytes accessed | tf_op | source)
XLA Modules:
  0.0 286.2 jit_solution(4251869853872702693)
XLA Ops:
  1.7 3.0 %collective-permute-start = (bf16[1,16,2,32,128]{4,3,2,1,0:T(8,128)(2,1)S(1)}, bf16[1,16,2,32,128]{4,3,2,1,0:T(8,128)(2,1)S(1)}, u32[]{:S(2)}, u32[]{:S(2)}) collective-permute-start(bf16[1,16,2,32,128]{4,3,2,1,0:T(8,128)(2,1)S(1)} %slice.88.refs_1_.refs_2_), channel_id=1, source_target_pairs={{0,16},{8,24},{16,0},{24,8},{1,17},{9,25},{17,1},{25,9},{2,18},{10... | collective-permute-start | bytes 786440 | tf_op jit(solution)/shard_map/ppermute | solution.py:332
  4.7 1.3 slice.87.refs_1_.refs_2_
  6.0 5.0 %collective-permute-done.refs_3_.refs_4_ = bf16[1,16,2,32,128]{4,3,2,1,0:T(8,128)(2,1)S(1)} collective-permute-done((bf16[1,16,2,32,128]{4,3,2,1,0:T(8,128)(2,1)S(1)}, bf16[1,16,2,32,128]{4,3,2,1,0:T(8,128)(2,1)S(1)}, u32[]{:S(2)}, u32[]{:S(2)}) %collective-permute-start) | collective-permute-done | bytes 262176 | tf_op jit(solution)/shard_map/ppermute | solution.py:332
  11.0 1.7 collective-permute-start.2
  13.2 1.2 slice.89.refs_2_.refs_1_
  15.2 20.1 %collective-permute-done.2.refs_3_.refs_4_ = bf16[4,16,2,32,128]{4,3,2,1,0:T(8,128)(2,1)S(1)} collective-permute-done((bf16[4,16,2,32,128]{4,3,2,1,0:T(8,128)(2,1)S(1)}, bf16[4,16,2,32,128]{4,3,2,1,0:T(8,128)(2,1)S(1)}, u32[]{:S(2)}, u32[]{:S(2)}) %collective-permute-start.2) | collective-permute-done | bytes 1048608 | tf_op jit(solution)/shard_map/ppermute | solution.py:332
  35.3 1.4 collective-permute-start.8
  36.8 2.6 collective-permute-start.12
  39.3 15.9 %collective-permute-done.8.refs_4_.refs_3_ = bf16[3,16,2,32,128]{4,3,2,1,0:T(8,128)(2,1)S(1)} collective-permute-done((bf16[3,16,2,32,128]{4,3,2,1,0:T(8,128)(2,1)S(1)}, bf16[3,16,2,32,128]{4,3,2,1,0:T(8,128)(2,1)S(1)}, u32[]{:S(2)}, u32[]{:S(2)}) %collective-permute-start.8) | collective-permute-done | bytes 786464 | tf_op jit(solution)/shard_map/ppermute | solution.py:332
  55.4 2.2 shard_map.75
  57.6 1.5 collective-permute-start.4
  59.1 3.8 %collective-permute-done.12.refs_1_ = bf16[128,2048]{1,0:T(8,128)(2,1)S(1)} collective-permute-done((bf16[128,2048]{1,0:T(8,128)(2,1)S(1)}, bf16[128,2048]{1,0:T(8,128)(2,1)S(1)}, u32[]{:S(2)}, u32[]{:S(2)}) %collective-permute-start.12) | collective-permute-done | bytes 524320 | tf_op jit(solution)/shard_map/ppermute | solution.py:15
  63.6 8.4 %collective-permute-done.4.refs_1_.refs_2_ = bf16[128,2048]{1,0:T(8,128)(2,1)S(1)} collective-permute-done((bf16[128,2048]{1,0:T(8,128)(2,1)S(1)}, bf16[128,2048]{1,0:T(8,128)(2,1)S(1)}, u32[]{:S(2)}, u32[]{:S(2)}) %collective-permute-start.4) | collective-permute-done | bytes 524320 | tf_op jit(solution)/shard_map/ppermute | solution.py:15
  72.8 3.3 %collective-permute-done.13.refs_4_ = bf16[2,16,2,32,128]{4,3,2,1,0:T(8,128)(2,1)S(1)} collective-permute-done((bf16[2,16,2,32,128]{4,3,2,1,0:T(8,128)(2,1)S(1)}, bf16[2,16,2,32,128]{4,3,2,1,0:T(8,128)(2,1)S(1)}, u32[]{:S(2)}, u32[]{:S(2)}) %collective-permute-start.13) | collective-permute-done | bytes 524320 | tf_op jit(solution)/shard_map/ppermute | solution.py:332
  77.3 1.2 collective-permute-start.10
  80.1 1.3 collective-permute-start.20
  81.4 10.7 %collective-permute-done.10.refs_1_.refs_3_ = bf16[128,2048]{1,0:T(8,128)(2,1)S(1)} collective-permute-done((bf16[128,2048]{1,0:T(8,128)(2,1)S(1)}, bf16[128,2048]{1,0:T(8,128)(2,1)S(1)}, u32[]{:S(2)}, u32[]{:S(2)}) %collective-permute-start.10) | collective-permute-done | bytes 524320 | tf_op jit(solution)/shard_map/ppermute | solution.py:15
  92.9 6.8 %collective-permute-done.15.refs_3_.refs_4_ = bf16[4,16,2,32,128]{4,3,2,1,0:T(8,128)(2,1)S(1)} collective-permute-done((bf16[4,16,2,32,128]{4,3,2,1,0:T(8,128)(2,1)S(1)}, bf16[4,16,2,32,128]{4,3,2,1,0:T(8,128)(2,1)S(1)}, u32[]{:S(2)}, u32[]{:S(2)}) %collective-permute-start.15) | collective-permute-done | bytes 1048608 | tf_op jit(solution)/shard_map/ppermute | solution.py:332
  100.2 2.2 collective-permute-done.20.refs_1_
  103.0 1.5 collective-permute-start.21
  104.5 21.7 %collective-permute-done.11.refs_1_ = bf16[128,2048]{1,0:T(8,128)(2,1)S(1)} collective-permute-done((bf16[128,2048]{1,0:T(8,128)(2,1)S(1)}, bf16[128,2048]{1,0:T(8,128)(2,1)S(1)}, u32[]{:S(2)}, u32[]{:S(2)}) %collective-permute-start.11) | collective-permute-done | bytes 524320 | tf_op jit(solution)/shard_map/ppermute | solution.py:15
  127.0 2.3 shard_map.83
  130.7 3.2 %shard_map.80 = (bf16[128,2048]{1,0:T(8,128)(2,1)S(1)}, bf16[128,2048]{1,0:T(8,128)(2,1)S(1)}, bf16[128,2048]{1,0:T(8,128)(2,1)S(1)}, bf16[128,2048]{1,0:T(8,128)(2,1)}) custom-call(bf16[128,2048]{1,0:T(8,128)(2,1)S(1)} %get-tuple-element.117.refs_0_, bf16[4,16,2,32,128]{4,3,2,1,0:T(8,128)(2,1)S(1)} %slice.90.refs_1_.refs_2_, ...), custom_call_target="tpu_custom_call" | custom-call | flops 1 | bytes 1 | tf_op jit(solution)/shard_map/pallas_call | solution.py:284
  134.9 1.4 shard_map.86
  137.5 1.5 collective-permute-start.17
  141.8 9.8 %collective-permute-done.17.refs_1_.refs_2_ = bf16[128,2048]{1,0:T(8,128)(2,1)S(1)} collective-permute-done((bf16[128,2048]{1,0:T(8,128)(2,1)}, bf16[128,2048]{1,0:T(8,128)(2,1)S(1)}, u32[]{:S(2)}, u32[]{:S(2)}) %collective-permute-start.17) | collective-permute-done | bytes 524320 | tf_op jit(solution)/shard_map/ppermute | solution.py:15
  151.6 12.8 %collective-permute-done.22.refs_1_ = bf16[128,2048]{1,0:T(8,128)(2,1)S(1)} collective-permute-done((bf16[128,2048]{1,0:T(8,128)(2,1)S(1)}, bf16[128,2048]{1,0:T(8,128)(2,1)S(1)}, u32[]{:S(2)}, u32[]{:S(2)}) %collective-permute-start.22) | collective-permute-done | bytes 524320 | tf_op jit(solution)/shard_map/ppermute | solution.py:15
  164.4 1.6 shard_map.87.refs_0_.refs_1_
  166.8 2.1 collective-permute-start.29
  168.8 1.5 collective-permute-start.27
  170.3 10.5 %collective-permute-done.25.refs_1_.refs_3_ = bf16[128,2048]{1,0:T(8,128)(2,1)S(1)} collective-permute-done((bf16[128,2048]{1,0:T(8,128)(2,1)S(1)}, bf16[128,2048]{1,0:T(8,128)(2,1)S(1)}, u32[]{:S(2)}, u32[]{:S(2)}) %collective-permute-start.25) | collective-permute-done | bytes 524320 | tf_op jit(solution)/shard_map/ppermute | solution.py:15
  182.2 9.0 %collective-permute-done.29.refs_1_ = bf16[128,2048]{1,0:T(8,128)(2,1)S(1)} collective-permute-done((bf16[128,2048]{1,0:T(8,128)(2,1)S(1)}, bf16[128,2048]{1,0:T(8,128)(2,1)S(1)}, u32[]{:S(2)}, u32[]{:S(2)}) %collective-permute-start.29) | collective-permute-done | bytes 524320 | tf_op jit(solution)/shard_map/ppermute | solution.py:15
  194.3 1.1 collective-permute-done.30
  195.4 1.2 fusion.8
  196.6 22.4 %collective-permute-done.26.refs_1_ = bf16[128,2048]{1,0:T(8,128)(2,1)S(1)} collective-permute-done((bf16[128,2048]{1,0:T(8,128)(2,1)S(1)}, bf16[128,2048]{1,0:T(8,128)(2,1)S(1)}, u32[]{:S(2)}, u32[]{:S(2)}) %collective-permute-start.26) | collective-permute-done | bytes 524320 | tf_op jit(solution)/shard_map/ppermute | solution.py:15
  219.0 3.3 %shard_map.93 = (bf16[128,2048]{1,0:T(8,128)(2,1)S(1)}, bf16[128,2048]{1,0:T(8,128)(2,1)S(1)}, bf16[128,2048]{1,0:T(8,128)(2,1)S(1)}, bf16[128,2048]{1,0:T(8,128)(2,1)S(1)}, bf16[128,2048]{1,0:T(8,128)(2,1)}) custom-call(f32[128,2048]{1,0:T(8,128)S(1)} %get-tuple-element.97.refs_0_, bf16[128,2048]{1,0:T(8,128)(2,1)S(1)} %collective-permute-done.31.refs_1_, ...), custom_call_target="tpu_custom_call" | custom-call | flops 1 | bytes 1 | tf_op jit(solution)/shard_map/pallas_call | solution.py:303
  222.4 1.4 shard_map.94
  223.9 1.9 shard_map.95
  227.2 2.3 collective-permute-done.35
  229.7 1.6 collective-permute-start.36
  231.9 1.6 collective-permute-start.38
  234.0 21.8 %collective-permute-done.33 = bf16[2,16,2,32,128]{4,3,2,1,0:T(8,128)(2,1)S(1)} collective-permute-done((bf16[2,16,2,32,128]{4,3,2,1,0:T(8,128)(2,1)S(1)}, bf16[2,16,2,32,128]{4,3,2,1,0:T(8,128)(2,1)S(1)}, u32[]{:S(2)}, u32[]{:S(2)}) %collective-permute-start.33) | collective-permute-done | bytes 524320 | tf_op jit(solution)/shard_map/ppermute | solution.py:332
  255.8 1.5 collective-permute-start.34
  258.0 1.4 shard_map.89
  259.3 2.1 collective-permute-done.38
  261.8 2.5 pad_maximum_fusion.1
  264.6 18.4 %collective-permute-done.34 = bf16[4,16,2,32,128]{4,3,2,1,0:T(8,128)(2,1)S(1)} collective-permute-done((bf16[4,16,2,32,128]{4,3,2,1,0:T(8,128)(2,1)S(1)}, bf16[4,16,2,32,128]{4,3,2,1,0:T(8,128)(2,1)S(1)}, u32[]{:S(2)}, u32[]{:S(2)}) %collective-permute-start.34) | collective-permute-done | bytes 1048608 | tf_op jit(solution)/shard_map/ppermute | solution.py:332
  283.7 2.5 pad_maximum_fusion
  (162 shorter events, 24.9 us)
Async XLA Ops:
  1.7 9.3 %collective-permute-start = (bf16[1,16,2,32,128]{4,3,2,1,0:T(8,128)(2,1)S(1)}, bf16[1,16,2,32,128]{4,3,2,1,0:T(8,128)(2,1)S(1)}, u32[]{:S(2)}, u32[]{:S(2)}) collective-permute-start(bf16[1,16,2,32,128]{4,3,2,1,0:T(8,128)(2,1)S(1)} %slice.88.refs_1_.refs_2_), channel_id=1, source_target_pairs={{0,16},{8,24},{16,0},{24,8},{1,17},{9,25},{17,1},{25,9},{2,18},{10... | collective-permute-start | bytes 786440 | tf_op jit(solution)/shard_map/ppermute | solution.py:332
  6.0 49.3 %copy-start.35 = (bf16[7,16,2,32,128]{4,3,2,1,0:T(8,128)(2,1)S(1)}, bf16[7,16,2,32,128]{4,3,2,1,0:T(8,128)(2,1)}, u32[]{:S(2)}) copy-start(bf16[7,16,2,32,128]{4,3,2,1,0:T(8,128)(2,1)} %param.7) | copy-start | bytes 5505028
  6.0 49.4 %copy-start.9 = (bf16[128,2048]{1,0:T(8,128)(2,1)S(1)}, bf16[128,2048]{1,0:T(8,128)(2,1)}, u32[]{:S(2)}) copy-start(bf16[128,2048]{1,0:T(8,128)(2,1)} %refs_0_.5) | copy-start | bytes 1572868
  11.0 44.4 %copy-start.11 = (bf16[1,16,2,32,128]{4,3,2,1,0:T(8,128)(2,1)}, bf16[1,16,2,32,128]{4,3,2,1,0:T(8,128)(2,1)S(1)}, u32[]{:S(2)}) copy-start(bf16[1,16,2,32,128]{4,3,2,1,0:T(8,128)(2,1)S(1)} %collective-permute-done.refs_3_.refs_4_) | copy-start | bytes 786436
  11.0 24.3 %collective-permute-start.2 = (bf16[4,16,2,32,128]{4,3,2,1,0:T(8,128)(2,1)S(1)}, bf16[4,16,2,32,128]{4,3,2,1,0:T(8,128)(2,1)S(1)}, u32[]{:S(2)}, u32[]{:S(2)}) collective-permute-start(bf16[4,16,2,32,128]{4,3,2,1,0:T(8,128)(2,1)S(1)} %slice.87.refs_1_.refs_2_), channel_id=1, source_target_pairs={{0,16},{8,24},{16,0},{24,8},{1,17},{9,25},{17,1},{25,9},{2,18},{10... | collective-permute-start | bytes 3145736 | tf_op jit(solution)/shard_map/ppermute | solution.py:332
  12.7 1.8 collective-permute-start.5
  12.7 1.9 collective-permute-start.6
  14.4 40.9 %collective-permute-start.1 = (bf16[4,16,2,32,128]{4,3,2,1,0:T(8,128)(2,1)S(1)}, bf16[4,16,2,32,128]{4,3,2,1,0:T(8,128)(2,1)S(1)}, u32[]{:S(2)}, u32[]{:S(2)}) collective-permute-start(bf16[4,16,2,32,128]{4,3,2,1,0:T(8,128)(2,1)S(1)} %slice.87.refs_1_.refs_2_), channel_id=1, source_target_pairs={{0,8},{8,0},{16,24},{24,16},{1,9},{9,1},{17,25},{25,17},{2,10},{10... | collective-permute-start | bytes 3145736 | tf_op jit(solution)/shard_map/ppermute | solution.py:332
  14.5 43.1 %copy-start.13 = (bf16[1,16,2,32,128]{4,3,2,1,0:T(8,128)(2,1)}, bf16[1,16,2,32,128]{4,3,2,1,0:T(8,128)(2,1)S(1)}, u32[]{:S(2)}) copy-start(bf16[1,16,2,32,128]{4,3,2,1,0:T(8,128)(2,1)S(1)} %collective-permute-done.5.refs_2_.refs_3_) | copy-start | bytes 786436
  14.6 42.9 %copy-start.15 = (bf16[1,16,2,32,128]{4,3,2,1,0:T(8,128)(2,1)}, bf16[1,16,2,32,128]{4,3,2,1,0:T(8,128)(2,1)S(1)}, u32[]{:S(2)}) copy-start(bf16[1,16,2,32,128]{4,3,2,1,0:T(8,128)(2,1)S(1)} %collective-permute-done.6.refs_4_.refs_5_) | copy-start | bytes 786436
  35.3 20.0 %collective-permute-start.3 = (bf16[4,16,2,32,128]{4,3,2,1,0:T(8,128)(2,1)S(1)}, bf16[4,16,2,32,128]{4,3,2,1,0:T(8,128)(2,1)S(1)}, u32[]{:S(2)}, u32[]{:S(2)}) collective-permute-start(bf16[4,16,2,32,128]{4,3,2,1,0:T(8,128)(2,1)S(1)} %collective-permute-done.2.refs_3_.refs_4_), channel_id=1, source_target_pairs={{0,8},{8,0},{16,24},{24,16},{1,9},{9,1},{17,25},{25,17},{2,10},{10... | collective-permute-start | bytes 3145736 | tf_op jit(solution)/shard_map/ppermute | solution.py:332
  35.3 20.0 %collective-permute-start.8 = (bf16[3,16,2,32,128]{4,3,2,1,0:T(8,128)(2,1)S(1)}, bf16[3,16,2,32,128]{4,3,2,1,0:T(8,128)(2,1)S(1)}, u32[]{:S(2)}, u32[]{:S(2)}) collective-permute-start(bf16[3,16,2,32,128]{4,3,2,1,0:T(8,128)(2,1)S(1)} %slice.89.refs_2_.refs_1_), channel_id=1, source_target_pairs={{0,16},{8,24},{16,0},{24,8},{1,17},{9,25},{17,1},{25,9},{2,18},{10... | collective-permute-start | bytes 2359304 | tf_op jit(solution)/shard_map/ppermute | solution.py:332
  36.8 26.2 %collective-permute-start.12 = (bf16[128,2048]{1,0:T(8,128)(2,1)S(1)}, bf16[128,2048]{1,0:T(8,128)(2,1)S(1)}, u32[]{:S(2)}, u32[]{:S(2)}) collective-permute-start(bf16[128,2048]{1,0:T(8,128)(2,1)S(1)} %get-tuple-element.64), channel_id=1, source_target_pairs={{0,4},{1,5},{2,6},{3,7},{4,0},{5,1},{6,2},{7,3},{8,12},{9,13},{10,... | collective-permute-start | bytes 1572872 | tf_op jit(solution)/shard_map/ppermute | solution.py:15
  39.3 24.3 %collective-permute-start.7 = (bf16[3,16,2,32,128]{4,3,2,1,0:T(8,128)(2,1)S(1)}, bf16[3,16,2,32,128]{4,3,2,1,0:T(8,128)(2,1)S(1)}, u32[]{:S(2)}, u32[]{:S(2)}) collective-permute-start(bf16[3,16,2,32,128]{4,3,2,1,0:T(8,128)(2,1)S(1)} %slice.89.refs_2_.refs_1_), channel_id=1, source_target_pairs={{0,8},{8,0},{16,24},{24,16},{1,9},{9,1},{17,25},{25,17},{2,10},{10... | collective-permute-start | bytes 2359304 | tf_op jit(solution)/shard_map/ppermute | solution.py:332
  55.3 8.3 %collective-permute-start.9 = (bf16[3,16,2,32,128]{4,3,2,1,0:T(8,128)(2,1)S(1)}, bf16[3,16,2,32,128]{4,3,2,1,0:T(8,128)(2,1)S(1)}, u32[]{:S(2)}, u32[]{:S(2)}) collective-permute-start(bf16[3,16,2,32,128]{4,3,2,1,0:T(8,128)(2,1)S(1)} %collective-permute-done.8.refs_4_.refs_3_), channel_id=1, source_target_pairs={{0,8},{8,0},{16,24},{24,16},{1,9},{9,1},{17,25},{25,17},{2,10},{10... | collective-permute-start | bytes 2359304 | tf_op jit(solution)/shard_map/ppermute | solution.py:332
  57.6 14.4 %collective-permute-start.4 = (bf16[128,2048]{1,0:T(8,128)(2,1)S(1)}, bf16[128,2048]{1,0:T(8,128)(2,1)S(1)}, u32[]{:S(2)}, u32[]{:S(2)}) collective-permute-start(bf16[128,2048]{1,0:T(8,128)(2,1)S(1)} %get-tuple-element.61.refs_0_), channel_id=1, source_target_pairs={{0,1},{1,0},{2,3},{3,2},{4,5},{5,4},{6,7},{7,6},{8,9},{9,8},{10,11... | collective-permute-start | bytes 1572872 | tf_op jit(solution)/shard_map/ppermute | solution.py:15
  62.9 13.2 %collective-permute-start.13 = (bf16[2,16,2,32,128]{4,3,2,1,0:T(8,128)(2,1)S(1)}, bf16[2,16,2,32,128]{4,3,2,1,0:T(8,128)(2,1)S(1)}, u32[]{:S(2)}, u32[]{:S(2)}) collective-permute-start(bf16[2,16,2,32,128]{4,3,2,1,0:T(8,128)(2,1)S(1)} %slice.91.refs_2_), channel_id=1, source_target_pairs={{0,16},{8,24},{16,0},{24,8},{1,17},{9,25},{17,1},{25,9},{2,18},{10... | collective-permute-start | bytes 1572872 | tf_op jit(solution)/shard_map/ppermute | solution.py:332
  76.2 23.6 %collective-permute-start.15 = (bf16[4,16,2,32,128]{4,3,2,1,0:T(8,128)(2,1)S(1)}, bf16[4,16,2,32,128]{4,3,2,1,0:T(8,128)(2,1)S(1)}, u32[]{:S(2)}, u32[]{:S(2)}) collective-permute-start(bf16[4,16,2,32,128]{4,3,2,1,0:T(8,128)(2,1)S(1)} %slice.90.refs_1_.refs_2_), channel_id=1, source_target_pairs={{0,16},{8,24},{16,0},{24,8},{1,17},{9,25},{17,1},{25,9},{2,18},{10... | collective-permute-start | bytes 3145736 | tf_op jit(solution)/shard_map/ppermute | solution.py:332
  76.8 1.9 collective-permute-start.18
  76.8 2.7 collective-permute-start.19
  77.3 14.8 %collective-permute-start.10 = (bf16[128,2048]{1,0:T(8,128)(2,1)S(1)}, bf16[128,2048]{1,0:T(8,128)(2,1)S(1)}, u32[]{:S(2)}, u32[]{:S(2)}) collective-permute-start(bf16[128,2048]{1,0:T(8,128)(2,1)S(1)} %shard_map.77.refs_0_.refs_1_), channel_id=1, source_target_pairs={{0,2},{1,3},{2,0},{3,1},{4,6},{5,7},{6,4},{7,5},{8,10},{9,11},{10,... | collective-permute-start | bytes 1572872 | tf_op jit(solution)/shard_map/ppermute | solution.py:15
  78.5 48.5 %collective-permute-start.14 = (bf16[4,16,2,32,128]{4,3,2,1,0:T(8,128)(2,1)S(1)}, bf16[4,16,2,32,128]{4,3,2,1,0:T(8,128)(2,1)S(1)}, u32[]{:S(2)}, u32[]{:S(2)}) collective-permute-start(bf16[4,16,2,32,128]{4,3,2,1,0:T(8,128)(2,1)S(1)} %slice.90.refs_1_.refs_2_), channel_id=1, source_target_pairs={{0,8},{8,0},{16,24},{24,16},{1,9},{9,1},{17,25},{25,17},{2,10},{10... | collective-permute-start | bytes 3145736 | tf_op jit(solution)/shard_map/ppermute | solution.py:332
  80.1 22.3 %collective-permute-start.20 = (bf16[128,2048]{1,0:T(8,128)(2,1)S(1)}, bf16[128,2048]{1,0:T(8,128)(2,1)S(1)}, u32[]{:S(2)}, u32[]{:S(2)}) collective-permute-start(bf16[128,2048]{1,0:T(8,128)(2,1)S(1)} %get-tuple-element.70), channel_id=1, source_target_pairs={{0,2},{1,3},{2,0},{3,1},{4,6},{5,7},{6,4},{7,5},{8,10},{9,11},{10,... | collective-permute-start | bytes 1572872 | tf_op jit(solution)/shard_map/ppermute | solution.py:15
  99.7 27.3 %collective-permute-start.16 = (bf16[4,16,2,32,128]{4,3,2,1,0:T(8,128)(2,1)S(1)}, bf16[4,16,2,32,128]{4,3,2,1,0:T(8,128)(2,1)S(1)}, u32[]{:S(2)}, u32[]{:S(2)}) collective-permute-start(bf16[4,16,2,32,128]{4,3,2,1,0:T(8,128)(2,1)S(1)} %collective-permute-done.15.refs_3_.refs_4_), channel_id=1, source_target_pairs={{0,8},{8,0},{16,24},{24,16},{1,9},{9,1},{17,25},{25,17},{2,10},{10... | collective-permute-start | bytes 3145736 | tf_op jit(solution)/shard_map/ppermute | solution.py:332
  99.7 26.5 %collective-permute-start.11 = (bf16[128,2048]{1,0:T(8,128)(2,1)S(1)}, bf16[128,2048]{1,0:T(8,128)(2,1)S(1)}, u32[]{:S(2)}, u32[]{:S(2)}) collective-permute-start(bf16[128,2048]{1,0:T(8,128)(2,1)S(1)} %shard_map.78.refs_0_), channel_id=1, source_target_pairs={{0,4},{1,5},{2,6},{3,7},{4,0},{5,1},{6,2},{7,3},{8,12},{9,13},{10,... | collective-permute-start | bytes 1572872 | tf_op jit(solution)/shard_map/ppermute | solution.py:15
  103.0 24.0 %collective-permute-start.21 = (bf16[128,2048]{1,0:T(8,128)(2,1)S(1)}, bf16[128,2048]{1,0:T(8,128)(2,1)S(1)}, u32[]{:S(2)}, u32[]{:S(2)}) collective-permute-start(bf16[128,2048]{1,0:T(8,128)(2,1)S(1)} %get-tuple-element.72), channel_id=1, source_target_pairs={{0,1},{1,0},{2,3},{3,2},{4,5},{5,4},{6,7},{7,6},{8,9},{9,8},{10,11... | collective-permute-start | bytes 1572872 | tf_op jit(solution)/shard_map/ppermute | solution.py:15
  136.3 4.2 %collective-permute-start.24 = (bf16[2,4,16,2,32,128]{5,4,3,2,1,0:T(8,128)(2,1)S(1)}, bf16[2,4,16,2,32,128]{5,4,3,2,1,0:T(8,128)(2,1)S(1)}, u32[]{:S(2)}, u32[]{:S(2)}) collective-permute-start(bf16[2,4,16,2,32,128]{5,4,3,2,1,0:T(8,128)(2,1)S(1)} %get-tuple-element.85), channel_id=1, source_target_pairs={{0,8},{8,0},{16,24},{24,16},{1,9},{9,1},{17,25},{25,17},{2,10},{10... | collective-permute-start | bytes 6291464 | tf_op jit(solution)/shard_map/ppermute | solution.py:332
  136.9 4.7 %collective-permute-start.23 = (bf16[2,1,16,2,32,128]{5,4,3,2,1,0:T(8,128)(2,1)S(1)}, bf16[2,1,16,2,32,128]{5,4,3,2,1,0:T(8,128)(2,1)S(1)}, u32[]{:S(2)}, u32[]{:S(2)}) collective-permute-start(bf16[2,1,16,2,32,128]{5,4,3,2,1,0:T(8,128)(2,1)S(1)} %get-tuple-element.76), channel_id=1, source_target_pairs={{0,8},{8,0},{16,24},{24,16},{1,9},{9,1},{17,25},{25,17},{2,10},{10... | collective-permute-start | bytes 1572872 | tf_op jit(solution)/shard_map/ppermute | solution.py:332
  137.5 14.1 %collective-permute-start.17 = (bf16[128,2048]{1,0:T(8,128)(2,1)}, bf16[128,2048]{1,0:T(8,128)(2,1)S(1)}, u32[]{:S(2)}, u32[]{:S(2)}) collective-permute-start(bf16[128,2048]{1,0:T(8,128)(2,1)} %get-tuple-element.68.refs_0_), channel_id=1, source_target_pairs={{0,1},{1,0},{2,3},{3,2},{4,5},{5,4},{6,7},{7,6},{8,9},{9,8},{10,11... | collective-permute-start | bytes 1572872 | tf_op jit(solution)/shard_map/ppermute | solution.py:15
  139.6 24.8 %collective-permute-start.22 = (bf16[128,2048]{1,0:T(8,128)(2,1)S(1)}, bf16[128,2048]{1,0:T(8,128)(2,1)S(1)}, u32[]{:S(2)}, u32[]{:S(2)}) collective-permute-start(bf16[128,2048]{1,0:T(8,128)(2,1)S(1)} %get-tuple-element.74), channel_id=1, source_target_pairs={{0,4},{1,5},{2,6},{3,7},{4,0},{5,1},{6,2},{7,3},{8,12},{9,13},{10,... | collective-permute-start | bytes 1572872 | tf_op jit(solution)/shard_map/ppermute | solution.py:15
  141.0 40.4 %collective-permute-start.28 = (bf16[4,16,2,32,128]{4,3,2,1,0:T(8,128)(2,1)S(1)}, bf16[4,16,2,32,128]{4,3,2,1,0:T(8,128)(2,1)S(1)}, u32[]{:S(2)}, u32[]{:S(2)}) collective-permute-start(bf16[4,16,2,32,128]{4,3,2,1,0:T(8,128)(2,1)S(1)} %fusion.6), channel_id=1, source_target_pairs={{0,16},{8,24},{16,0},{24,8},{1,17},{9,25},{17,1},{25,9},{2,18},{10... | collective-permute-start | bytes 3145736 | tf_op jit(solution)/shard_map/ppermute | solution.py:332
  141.7 24.3 %copy-start.40 = (bf16[2,1,16,2,32,128]{5,4,3,2,1,0:T(8,128)(2,1)}, bf16[2,1,16,2,32,128]{5,4,3,2,1,0:T(8,128)(2,1)S(1)}, u32[]{:S(2)}) copy-start(bf16[2,1,16,2,32,128]{5,4,3,2,1,0:T(8,128)(2,1)S(1)} %collective-permute-done.23) | copy-start | bytes 1572868
  166.0 14.8 %collective-permute-start.25 = (bf16[128,2048]{1,0:T(8,128)(2,1)S(1)}, bf16[128,2048]{1,0:T(8,128)(2,1)S(1)}, u32[]{:S(2)}, u32[]{:S(2)}) collective-permute-start(bf16[128,2048]{1,0:T(8,128)(2,1)S(1)} %shard_map.87.refs_0_.refs_1_), channel_id=1, source_target_pairs={{0,2},{1,3},{2,0},{3,1},{4,6},{5,7},{6,4},{7,5},{8,10},{9,11},{10,... | collective-permute-start | bytes 1572872 | tf_op jit(solution)/shard_map/ppermute | solution.py:15
  166.8 24.4 %collective-permute-start.29 = (bf16[128,2048]{1,0:T(8,128)(2,1)S(1)}, bf16[128,2048]{1,0:T(8,128)(2,1)S(1)}, u32[]{:S(2)}, u32[]{:S(2)}) collective-permute-start(bf16[128,2048]{1,0:T(8,128)(2,1)S(1)} %get-tuple-element.91), channel_id=1, source_target_pairs={{0,2},{1,3},{2,0},{3,1},{4,6},{5,7},{6,4},{7,5},{8,10},{9,11},{10,... | collective-permute-start | bytes 1572872 | tf_op jit(solution)/shard_map/ppermute | solution.py:15
  168.8 12.6 %collective-permute-start.27 = (bf16[1,16,2,32,128]{4,3,2,1,0:T(8,128)(2,1)S(1)}, bf16[1,16,2,32,128]{4,3,2,1,0:T(8,128)(2,1)S(1)}, u32[]{:S(2)}, u32[]{:S(2)}) collective-permute-start(bf16[1,16,2,32,128]{4,3,2,1,0:T(8,128)(2,1)S(1)} %fusion.10), channel_id=1, source_target_pairs={{0,16},{8,24},{16,0},{24,8},{1,17},{9,25},{17,1},{25,9},{2,18},{10... | collective-permute-start | bytes 786440 | tf_op jit(solution)/shard_map/ppermute | solution.py:332
  192.7 2.7 collective-permute-start.30
  192.8 26.2 %collective-permute-start.26 = (bf16[128,2048]{1,0:T(8,128)(2,1)S(1)}, bf16[128,2048]{1,0:T(8,128)(2,1)S(1)}, u32[]{:S(2)}, u32[]{:S(2)}) collective-permute-start(bf16[128,2048]{1,0:T(8,128)(2,1)S(1)} %shard_map.88.refs_0_), channel_id=1, source_target_pairs={{0,4},{1,5},{2,6},{3,7},{4,0},{5,1},{6,2},{7,3},{8,12},{9,13},{10,... | collective-permute-start | bytes 1572872 | tf_op jit(solution)/shard_map/ppermute | solution.py:15
  193.8 25.2 %collective-permute-start.31 = (bf16[128,2048]{1,0:T(8,128)(2,1)S(1)}, bf16[128,2048]{1,0:T(8,128)(2,1)S(1)}, u32[]{:S(2)}, u32[]{:S(2)}) collective-permute-start(bf16[128,2048]{1,0:T(8,128)(2,1)S(1)} %get-tuple-element.98), channel_id=1, source_target_pairs={{0,1},{1,0},{2,3},{3,2},{4,5},{5,4},{6,7},{7,6},{8,9},{9,8},{10,11... | collective-permute-start | bytes 1572872 | tf_op jit(solution)/shard_map/ppermute | solution.py:15
  195.4 26.9 %copy-start.38 = (bf16[2,2,16,2,32,128]{5,4,3,2,1,0:T(8,128)(2,1)}, bf16[2,2,16,2,32,128]{5,4,3,2,1,0:T(8,128)(2,1)S(1)}, u32[]{:S(2)}) copy-start(bf16[2,2,16,2,32,128]{5,4,3,2,1,0:T(8,128)(2,1)S(1)} %collective-permute-done.30) | copy-start | bytes 3145732
  223.8 9.7 %collective-permute-start.32 = (bf16[2,4,16,2,32,128]{5,4,3,2,1,0:T(8,128)(2,1)S(1)}, bf16[2,4,16,2,32,128]{5,4,3,2,1,0:T(8,128)(2,1)S(1)}, u32[]{:S(2)}, u32[]{:S(2)}) collective-permute-start(bf16[2,4,16,2,32,128]{5,4,3,2,1,0:T(8,128)(2,1)S(1)} %get-tuple-element.108), channel_id=1, source_target_pairs={{0,8},{8,0},{16,24},{24,16},{1,9},{9,1},{17,25},{25,17},{2,10},{10... | collective-permute-start | bytes 6291464 | tf_op jit(solution)/shard_map/ppermute | solution.py:332
  225.9 3.6 %collective-permute-start.35 = (bf16[2,2,16,2,32,128]{5,4,3,2,1,0:T(8,128)(2,1)S(1)}, bf16[2,2,16,2,32,128]{5,4,3,2,1,0:T(8,128)(2,1)S(1)}, u32[]{:S(2)}, u32[]{:S(2)}) collective-permute-start(bf16[2,2,16,2,32,128]{5,4,3,2,1,0:T(8,128)(2,1)S(1)} %get-tuple-element.113), channel_id=1, source_target_pairs={{0,8},{8,0},{16,24},{24,16},{1,9},{9,1},{17,25},{25,17},{2,10},{10... | collective-permute-start | bytes 3145736 | tf_op jit(solution)/shard_map/ppermute | solution.py:332
  226.9 4.9 %collective-permute-start.37 = (bf16[2,1,16,2,32,128]{5,4,3,2,1,0:T(8,128)(2,1)S(1)}, bf16[2,1,16,2,32,128]{5,4,3,2,1,0:T(8,128)(2,1)S(1)}, u32[]{:S(2)}, u32[]{:S(2)}) collective-permute-start(bf16[2,1,16,2,32,128]{5,4,3,2,1,0:T(8,128)(2,1)S(1)} %get-tuple-element.115), channel_id=1, source_target_pairs={{0,8},{8,0},{16,24},{24,16},{1,9},{9,1},{17,25},{25,17},{2,10},{10... | collective-permute-start | bytes 1572872 | tf_op jit(solution)/shard_map/ppermute | solution.py:332
  229.7 27.6 %copy-start.34 = (bf16[2,4,16,2,32,128]{5,4,3,2,1,0:T(8,128)(2,1)S(1)}, bf16[2,4,16,2,32,128]{5,4,3,2,1,0:T(8,128)(2,1)}, u32[]{:S(2)}) copy-start(bf16[2,4,16,2,32,128]{5,4,3,2,1,0:T(8,128)(2,1)} %copy-done.33) | copy-start | bytes 6291460
  229.7 27.6 %copy-start.37 = (bf16[4,16,2,32,128]{4,3,2,1,0:T(8,128)(2,1)S(1)}, bf16[4,16,2,32,128]{4,3,2,1,0:T(8,128)(2,1)}, u32[]{:S(2)}) copy-start(bf16[4,16,2,32,128]{4,3,2,1,0:T(8,128)(2,1)} %copy-done.36) | copy-start | bytes 3145732
  229.7 31.8 %collective-permute-start.36 = (bf16[2,16,2,32,128]{4,3,2,1,0:T(8,128)(2,1)S(1)}, bf16[2,16,2,32,128]{4,3,2,1,0:T(8,128)(2,1)S(1)}, u32[]{:S(2)}, u32[]{:S(2)}) collective-permute-start(bf16[2,16,2,32,128]{4,3,2,1,0:T(8,128)(2,1)S(1)} %fusion.9), channel_id=1, source_target_pairs={{0,16},{8,24},{16,0},{24,8},{1,17},{9,25},{17,1},{25,9},{2,18},{10... | collective-permute-start | bytes 1572872 | tf_op jit(solution)/shard_map/ppermute | solution.py:332
  231.3 24.5 %collective-permute-start.33 = (bf16[2,16,2,32,128]{4,3,2,1,0:T(8,128)(2,1)S(1)}, bf16[2,16,2,32,128]{4,3,2,1,0:T(8,128)(2,1)S(1)}, u32[]{:S(2)}, u32[]{:S(2)}) collective-permute-start(bf16[2,16,2,32,128]{4,3,2,1,0:T(8,128)(2,1)S(1)} %copy-done.42), channel_id=1, source_target_pairs={{0,16},{8,24},{16,0},{24,8},{1,17},{9,25},{17,1},{25,9},{2,18},{10... | collective-permute-start | bytes 1572872 | tf_op jit(solution)/shard_map/ppermute | solution.py:332
  231.9 29.5 %collective-permute-start.38 = (bf16[1,16,2,32,128]{4,3,2,1,0:T(8,128)(2,1)S(1)}, bf16[1,16,2,32,128]{4,3,2,1,0:T(8,128)(2,1)S(1)}, u32[]{:S(2)}, u32[]{:S(2)}) collective-permute-start(bf16[1,16,2,32,128]{4,3,2,1,0:T(8,128)(2,1)S(1)} %fusion.11), channel_id=1, source_target_pairs={{0,16},{8,24},{16,0},{24,8},{1,17},{9,25},{17,1},{25,9},{2,18},{10... | collective-permute-start | bytes 786440 | tf_op jit(solution)/shard_map/ppermute | solution.py:332
  255.8 27.3 %collective-permute-start.34 = (bf16[4,16,2,32,128]{4,3,2,1,0:T(8,128)(2,1)S(1)}, bf16[4,16,2,32,128]{4,3,2,1,0:T(8,128)(2,1)S(1)}, u32[]{:S(2)}, u32[]{:S(2)}) collective-permute-start(bf16[4,16,2,32,128]{4,3,2,1,0:T(8,128)(2,1)S(1)} %fusion.7), channel_id=1, source_target_pairs={{0,16},{8,24},{16,0},{24,8},{1,17},{9,25},{17,1},{25,9},{2,18},{10... | collective-permute-start | bytes 3145736 | tf_op jit(solution)/shard_map/ppermute | solution.py:332
  (36 other events, 284.1 us)
